TPU v7x, 256 devices: a whole 4x4x8 slice. The times are simulated.
256 devices in a mesh: fsdp: 32 (over x, y, core), expert: 8 (over z).
Axes of the slice: x: 4, y: 4, z: 8, core: 2. Of those that a mesh axis runs over, the one named last changes fastest.
Arguments:
- grads: bfloat16 [8, 7168, 2048], P(None, ('fsdp', 'expert')), may hold values from -6 to 6
- momentum: float32 [8, 7168, 2048], P(None, ('fsdp', 'expert')), may hold values from -6 to 6
- max_logits: float32 [256, 64], P(('fsdp', 'expert')), may hold values from 4 to 500
- q_weight: bfloat16 [1536, 12288], P('fsdp', 'expert'), may hold values from -6 to 6
- k_weight: bfloat16 [512, 8192], P('fsdp', 'expert'), may hold values from -6 to 6
Outputs:
- new_momentum: float32 [8, 7168, 2048], P(None, ('fsdp', 'expert'))
- step: bfloat16 [8, 7168, 2048], P(None, ('fsdp', 'expert'))
- q_clipped: bfloat16 [1536, 12288], P('fsdp', 'expert')
- k_clipped: bfloat16 [512, 8192], P('fsdp', 'expert')
All inputs are finite; a program needn't handle non-finite values. Where the computation divides by a largest or mean magnitude, that divisor is 1e-20 or more.
Results may differ from a plain program's by a relative error of at most 0.012.
Values may be sent and summed in bfloat16 or wider, within the bound.
No kernel may reach another device: no remote copies, remote signals or barrier semaphores. Data moves between devices by JAX's collectives and lax.ppermute only.
A program may use at most 128 MiB of HBM per device.

v0:
```python
import math

import jax
import jax.numpy as jnp
from jax import lax
from jax.experimental import pallas as pl
from jax.experimental.pallas import tpu as pltpu
from jax.sharding import Mesh, PartitionSpec as P

D = 7168
FF = 2048
NOPE = 128
ROPE = 64

decay_rate = 0.9
linear_coef = 3.4445
cubic_coef = -4.775
quintic_coef = 2.0315
clip_limit = 100.0
rms_match = 0.2

NX, NY, NC, NZ = 4, 4, 2, 8
BLK = 128
NB = FF // BLK
HALF = FF // 2
BAND = (NB // 2 + 1) * BLK
PADROWS = 32
KROWS = NZ * PADROWS
CUT = 512
TAIL = 384
PACKED = FF + (FF // CUT) * TAIL
SHARE = BLK // 4

MASS = pl.BlockSpec(memory_space=pltpu.VMEM)
SCALARS = pl.BlockSpec(memory_space=pltpu.SMEM)


def room(mib):
    return pltpu.CompilerParams(vmem_limit_bytes=mib * 1024 * 1024)


def low_rows(value):
    return lax.broadcasted_iota(jnp.int32, value.shape, 1) < 4


def pack(tiles):
    t0, t1, t2, t3 = tiles
    e2, e3 = t2[:, :, TAIL:], t3[:, :, TAIL:]
    moved = jnp.concatenate([pltpu.roll(e2, 4, 1), e2, pltpu.roll(e3, 4, 1)], axis=2)
    last = t3[:, :, :TAIL]
    last = jnp.where(low_rows(last), last, moved)
    head = jnp.concatenate([t0, t1], axis=1)
    tail = jnp.concatenate([t2[:, :, :TAIL], last], axis=1)
    return head.astype(jnp.bfloat16), tail.astype(jnp.bfloat16)


def unpack(head, tail):
    head, tail = head.astype(jnp.float32), tail.astype(jnp.float32)
    t2, last = tail[:, :8], tail[:, 8:]
    m0, m1, m2 = last[:, :, :BLK], last[:, :, BLK : 2 * BLK], last[:, :, 2 * BLK :]
    e2 = jnp.where(low_rows(m0), pltpu.roll(m0, 4, 1), m1)
    e3 = pltpu.roll(m2, 4, 1)
    t2 = jnp.concatenate([t2, e2], axis=2)
    t3 = jnp.concatenate([last, e3], axis=2)
    t3 = jnp.where(low_rows(t3), t3, 0.0)
    return head[:, :8], head[:, 8:], t2, t3


def head_columns(n):
    return pl.ds(pl.multiple_of(n * CUT, CUT), CUT)


def tail_columns(n):
    return pl.ds(pl.multiple_of(FF + n * TAIL, BLK), TAIL)


def direction_kernel(grads_ref, momentum_ref, new_ref, out_ref):
    n = pl.program_id(0)
    grads = grads_ref[...].astype(jnp.float32)
    new = decay_rate * momentum_ref[...] + grads
    new_ref[...] = new
    direction = grads + decay_rate * new
    rows, mats, columns = direction.shape
    direction = jnp.concatenate([direction, jnp.zeros((PADROWS - rows, mats, columns), jnp.float32)], axis=0)
    head, tail = pack([jnp.swapaxes(direction[8 * t : 8 * t + 8], 0, 1) for t in range(4)])
    out_ref[:, :, head_columns(n)] = head
    out_ref[:, :, tail_columns(n)] = tail


def find_direction(grads, momentum):
    rows, mats = grads.shape[:2]
    cut = pl.BlockSpec((rows, mats, CUT), lambda n: (0, 0, n))
    return pl.pallas_call(
        direction_kernel,
        grid=(FF // CUT,),
        out_shape=(
            jax.ShapeDtypeStruct(grads.shape, jnp.float32),
            jax.ShapeDtypeStruct((mats, 16, PACKED), jnp.bfloat16),
        ),
        in_specs=[cut, cut],
        out_specs=(cut, pl.BlockSpec((mats, 16, PACKED), lambda n: (0, 0, 0))),
        compiler_params=room(24),
        name="find_direction",
    )(grads, momentum)


def spread_kernel(packed_ref, out_ref):
    n = pl.program_id(0)
    tiles = unpack(packed_ref[:, :, head_columns(n)], packed_ref[:, :, tail_columns(n)])
    rows = jnp.concatenate([jnp.swapaxes(t, 0, 1) for t in tiles], axis=0)
    out_ref[...] = rows[: out_ref.shape[0]].astype(jnp.bfloat16)


def spread_step(packed, rows):
    return pl.pallas_call(
        spread_kernel,
        grid=(FF // CUT,),
        out_shape=jax.ShapeDtypeStruct((rows, NZ, FF), jnp.bfloat16),
        in_specs=[pl.BlockSpec((NZ, 16, PACKED), lambda n: (0, 0, 0))],
        out_specs=pl.BlockSpec((rows, NZ, CUT), lambda n: (0, 0, n)),
        compiler_params=room(16),
        name="spread_step",
    )(packed)


def gram_kernel(place_ref, mine_ref, other_ref, *refs):
    shares, (x_ref, rows_ref, band_ref) = refs[:8], refs[8:]
    x, y, core = place_ref[0], place_ref[1], place_ref[2]
    for n in range(FF // CUT):
        source = (n + 2 * core) % 4
        columns = pl.ds(n * CUT, CUT)
        for half, packed in enumerate((mine_ref, other_ref)):
            tiles = unpack(packed[:, :, head_columns(source)], packed[:, :, tail_columns(source)])
            rows = jnp.concatenate(tiles, axis=1).reshape(KROWS, CUT).astype(jnp.bfloat16)
            rows_ref[pl.ds(half * KROWS, KROWS), columns] = rows
            if half == 0:
                x_ref[:, columns] = rows
    for pair in range(NB // 4):
        left = rows_ref[:, pl.ds(pair * 2 * BLK, 2 * BLK)]
        right = rows_ref[:, pl.ds(pair * 2 * BLK, BAND + BLK)]
        product = lax.dot_general(
            left, right, (((0,), (0,)), ((), ())), preferred_element_type=jnp.float32
        ).astype(jnp.bfloat16)
        for sub in range(2):
            band_ref[pl.ds((pair * 2 + sub) * BLK, BLK), :] = product[
                sub * BLK : (sub + 1) * BLK, sub * BLK : sub * BLK + BAND
            ]
    for d in range(4):
        shares[d][...] = band_ref[pl.ds(pl.multiple_of(((x + d) % 4) * BLK, BLK), BLK), :]
        shares[4 + d][...] = band_ref[pl.ds(pl.multiple_of((4 + (y + d) % 4) * BLK, BLK), BLK), :]


def gram_band(place, mine, other):
    return pl.pallas_call(
        gram_kernel,
        out_shape=[jax.ShapeDtypeStruct((BLK, BAND), jnp.bfloat16)] * 8
        + [jax.ShapeDtypeStruct((KROWS, FF), jnp.bfloat16)],
        in_specs=[SCALARS, MASS, MASS],
        out_specs=[MASS] * 9,
        scratch_shapes=[
            pltpu.VMEM((2 * KROWS, FF), jnp.bfloat16),
            pltpu.VMEM((HALF, BAND), jnp.bfloat16),
        ],
        compiler_params=room(28),
        name="gram_band",
    )(place, mine, other)


def partial_kernel(place_ref, *refs):
    parts, outs = refs[:8], refs[8:]
    for kind in range(2):
        here = place_ref[1 - kind]
        for d in range(4):
            rows = pl.ds(pl.multiple_of(((here + d) % 4) * SHARE, SHARE), SHARE)
            total = sum(part[rows, :].astype(jnp.float32) for part in parts[4 * kind : 4 * kind + 4])
            outs[4 * kind + d][...] = total.astype(jnp.bfloat16)


def partial_sums(place, parts):
    return pl.pallas_call(
        partial_kernel,
        out_shape=[jax.ShapeDtypeStruct((SHARE, BAND), jnp.bfloat16)] * 8,
        in_specs=[SCALARS] + [MASS] * 8,
        out_specs=[MASS] * 8,
        compiler_params=room(16),
        name="partial_sums",
    )(place, *parts)


def total_kernel(*refs):
    parts, outs = refs[:8], refs[8:]
    for kind in range(2):
        total = sum(part[...].astype(jnp.float32) for part in parts[4 * kind : 4 * kind + 4])
        outs[kind][...] = total.astype(jnp.bfloat16)


def total_sums(parts):
    return pl.pallas_call(
        total_kernel,
        out_shape=[jax.ShapeDtypeStruct((SHARE, BAND), jnp.bfloat16)] * 2,
        in_specs=[MASS] * 8,
        out_specs=[MASS] * 2,
        compiler_params=room(16),
        name="total_sums",
    )(*parts)


def step_kernel(place_ref, x_ref, *refs):
    pieces = refs[:16]
    out_ref, band_ref, gram_ref, first_ref, round_ref = refs[16:]
    x, y, core = place_ref[0], place_ref[1], place_ref[2]
    for side in range(2):
        for kind in range(2):
            for outer in range(4):
                piece = pieces[side * 8 + kind * 4 + outer]
                for inner in range(4):
                    dx, dy = (inner, outer) if kind == 0 else (outer, inner)
                    sx, sy = (x + (4 - dx)) % 4, (y + (4 - dy)) % 4
                    share = sx * 4 + sy if kind == 0 else 16 + sy * 4 + sx
                    row = pl.multiple_of(side * HALF + share * SHARE, SHARE)
                    band_ref[pl.ds(row, SHARE), :] = piece[inner]
    for i in range(NB):
        block = band_ref[pl.ds(i * BLK, BLK), :]
        turned = block[:, BLK : BAND - BLK].T
        for d in range(NB // 2 + 1):
            j = (i + d) % NB
            gram_ref[pl.ds(i * BLK, BLK), pl.ds(j * BLK, BLK)] = block[:, d * BLK : (d + 1) * BLK]
            if 1 <= d < NB // 2:
                gram_ref[pl.ds(j * BLK, BLK), pl.ds(i * BLK, BLK)] = turned[(d - 1) * BLK : d * BLK]

    def add_rows(k, total):
        part = jnp.abs(gram_ref[pl.ds(pl.multiple_of(k * 64, 64), 64), :].astype(jnp.float32))
        return total + jnp.sum(part.reshape(8, 8, FF), axis=0)

    sums = lax.fori_loop(0, FF // 64, add_rows, jnp.zeros((8, FF), jnp.float32))
    bound = jnp.max(jnp.sum(sums, axis=0, keepdims=True))
    bound = jnp.full((1, 1), bound, jnp.float32)
    inverse = 1.0 / bound
    scale = rms_match * math.sqrt(max(D, FF)) / jnp.sqrt(bound)
    for n in range(FF // CUT):
        columns = pl.ds(n * CUT, CUT)
        first = jnp.dot(x_ref[...], gram_ref[:, columns], preferred_element_type=jnp.float32) * inverse
        first_ref[:, columns] = linear_coef * x_ref[:, columns].astype(jnp.float32) + cubic_coef * first
        round_ref[:, columns] = first.astype(jnp.bfloat16)
    for n in range(FF // CUT):
        columns = pl.ds(n * CUT, CUT)
        second = jnp.dot(round_ref[...], gram_ref[:, columns], preferred_element_type=jnp.float32) * inverse
        step = scale * (first_ref[:, columns] + quintic_coef * second)
        step = step.reshape(NZ, PADROWS, CUT)
        head, tail = pack([step[:, 8 * t : 8 * t + 8] for t in range(4)])
        target = (n + 2 * core) % 4
        out_ref[:, :, head_columns(target)] = head
        out_ref[:, :, tail_columns(target)] = tail


def finish(place, mine, pieces):
    return pl.pallas_call(
        step_kernel,
        out_shape=jax.ShapeDtypeStruct((NZ, 16, PACKED), jnp.bfloat16),
        in_specs=[SCALARS] + [MASS] * 17,
        out_specs=MASS,
        scratch_shapes=[
            pltpu.VMEM((FF, BAND), jnp.bfloat16),
            pltpu.VMEM((FF, FF), jnp.bfloat16),
            pltpu.VMEM((KROWS, FF), jnp.float32),
            pltpu.VMEM((KROWS, FF), jnp.bfloat16),
        ],
        compiler_params=room(40),
        name="finish",
    )(place, mine, *pieces)


def shift(value, axis, by, size):
    return lax.ppermute(value, axis, [(i, (i + by) % size) for i in range(size)])


def swap_cores(value):
    return lax.ppermute(value, "c", [(0, 1), (1, 0)])


def spread(value, axis):
    return [value] + [shift(value, axis, d, 4) for d in range(1, 4)]


def largest(value):
    for axis, size in (("c", NC), ("x", NX), ("y", NY), ("z", NZ)):
        by = 1
        while by < size:
            value = jnp.maximum(value, shift(value, axis, by, size))
            by *= 2
    return value


def body(grads, momentum, max_logits, q_weight, k_weight):
    x, y, core = lax.axis_index("x"), lax.axis_index("y"), lax.axis_index("c")
    place = jnp.stack([x, y, core]).astype(jnp.int32)
    rows = grads.shape[1]
    new_momentum, direction = find_direction(jnp.swapaxes(grads, 0, 1), jnp.swapaxes(momentum, 0, 1))
    new_momentum = jnp.swapaxes(new_momentum, 0, 1)
    owned = lax.all_to_all(direction, "z", split_axis=0, concat_axis=0, tiled=True)
    *shares, mine = gram_band(place, owned, swap_cores(owned))
    parts = [shares[0]] + [shift(shares[d], "x", d, 4) for d in range(1, 4)]
    parts += [shares[4]] + [shift(shares[4 + d], "y", d, 4) for d in range(1, 4)]
    shares = partial_sums(place, parts)
    parts = [shares[0]] + [shift(shares[d], "y", d, 4) for d in range(1, 4)]
    parts += [shares[4]] + [shift(shares[4 + d], "x", d, 4) for d in range(1, 4)]
    a, b = total_sums(parts)
    a = jnp.stack(spread(a, "x"))
    b = jnp.stack(spread(b, "y"))
    own = spread(a, "y") + spread(b, "x")
    other = [swap_cores(piece) for piece in own]
    step = finish(place, mine, own + other)
    step = lax.all_to_all(step, "z", split_axis=0, concat_axis=0, tiled=True)
    step = jnp.swapaxes(spread_step(step, rows), 0, 1)

    peak = largest(max_logits)[0]
    gamma = jnp.minimum(1.0, clip_limit / peak)
    root = jnp.sqrt(gamma)
    local_heads = k_weight.shape[1] // NOPE
    first_head = lax.axis_index("z") * local_heads
    gamma_mine = lax.dynamic_slice_in_dim(gamma, first_head, local_heads)
    root_mine = lax.dynamic_slice_in_dim(root, first_head, local_heads)
    q_factor = jnp.concatenate(
        [
            jnp.broadcast_to(root_mine[:, None], (local_heads, NOPE)),
            jnp.broadcast_to(gamma_mine[:, None], (local_heads, ROPE)),
        ],
        axis=1,
    )
    q_view = q_weight.reshape(q_weight.shape[0], local_heads, NOPE + ROPE).astype(jnp.float32)
    q_clipped = (q_view * q_factor[None]).astype(jnp.bfloat16).reshape(q_weight.shape)
    k_view = k_weight.reshape(k_weight.shape[0], local_heads, NOPE).astype(jnp.float32)
    k_clipped = (k_view * root_mine[None, :, None]).astype(jnp.bfloat16).reshape(k_weight.shape)
    return (new_momentum, step, q_clipped, k_clipped)


def solution(mesh):
    split = Mesh(mesh.devices.reshape(NX, NY, NC, NZ), ("x", "y", "c", "z"))
    rows = P(None, ("x", "y", "c", "z"), None)
    heads = P(("x", "y", "c"), "z")
    return jax.shard_map(
        body,
        mesh=split,
        in_specs=(rows, rows, P(("x", "y", "c", "z"), None), heads, heads),
        out_specs=(rows, rows, heads, heads),
        check_vma=False,
    )
```

profile of v0, /device:TPU:2, one launch (start us, length us, event | category | flops | bytes accessed | tf_op | source)
XLA Modules:
  0.0 167.1 jit_solution(9797555912279331435)
XLA Ops:
  3.3 2.1 %find_direction.1 = (f32[28,8,2048]{2,1,0:T(8,128)}, bf16[8,16,3584]{2,1,0:T(8,128)(2,1)S(1)}) custom-call(bf16[28,8,2048]{2,1,0:T(8,128)(2,1)S(1)} %bitcast.22, f32[28,8,2048]{2,1,0:T(8,128)S(1)} %bitcast.21), custom_call_target="tpu_custom_call" | custom-call | tf_op jit(solution)/shard_map/find_direction/pallas_call | solution.py:93
  5.4 34.2 %all_to_all.10.mine_ref = bf16[8,16,3584]{2,1,0:T(8,128)(2,1)S(1)} all-to-all(bf16[8,16,3584]{2,1,0:T(8,128)(2,1)S(1)} %get-tuple-element.26), channel_id=1, replica_groups=mesh['x'=4,'y'=4,'c'=2,'z'=8] {'z'}, dimensions={0} | all-to-all | bytes 1835008 | tf_op jit(solution)/shard_map/all_to_all | solution.py:300
  39.7 2.4 %collective-permute-done.other_ref = bf16[8,16,3584]{2,1,0:T(8,128)(2,1)S(1)} collective-permute-done((bf16[8,16,3584]{2,1,0:T(8,128)(2,1)S(1)}, bf16[8,16,3584]{2,1,0:T(8,128)(2,1)S(1)}, u32[]{:S(2)}, u32[]{:S(2)}) %collective-permute-start) | collective-permute-done | bytes 917536 | tf_op jit(solution)/shard_map/ppermute | solution.py:278
  42.1 2.3 %gram_band.1 = (bf16[128,1152]{1,0:T(8,128)(2,1)S(1)}, bf16[128,1152]{1,0:T(8,128)(2,1)S(1)}, bf16[128,1152]{1,0:T(8,128)(2,1)S(1)}, bf16[128,1152]{1,0:T(8,128)...) custom-call(s32[3]{0:T(128)S(1)} %pad_add_fusion.place_ref, ...), custom_call_target="tpu_custom_call" | custom-call | tf_op jit(solution)/shard_map/gram_band/pallas_call | solution.py:154
  47.1 2.2 %collective-permute-start.3 = (bf16[128,1152]{1,0:T(8,128)(2,1)S(1)}, bf16[128,1152]{1,0:T(8,128)(2,1)S(1)}, u32[]{:S(2)}, u32[]{:S(2)}) collective-permute-start(bf16[128,1152]{1,0:T(8,128)(2,1)S(1)} %get-tuple-element.31), channel_id=1, source_target_pairs={{0,192},{64,0},{128,64},{192,128},{1,193},{65,1},{129,65},{193,129... | collective-permute-start | bytes 884744 | tf_op jit(solution)/shard_map/ppermute | solution.py:274
  50.8 2.9 %collective-permute-start.5 = (bf16[128,1152]{1,0:T(8,128)(2,1)S(1)}, bf16[128,1152]{1,0:T(8,128)(2,1)S(1)}, u32[]{:S(2)}, u32[]{:S(2)}) collective-permute-start(bf16[128,1152]{1,0:T(8,128)(2,1)S(1)} %get-tuple-element.34), channel_id=1, source_target_pairs={{0,32},{16,48},{32,0},{48,16},{1,33},{17,49},{33,1},{49,17},{2,34}... | collective-permute-start | bytes 884744 | tf_op jit(solution)/shard_map/ppermute | solution.py:274
  54.3 3.0 %collective-permute-start.6 = (bf16[128,1152]{1,0:T(8,128)(2,1)S(1)}, bf16[128,1152]{1,0:T(8,128)(2,1)S(1)}, u32[]{:S(2)}, u32[]{:S(2)}) collective-permute-start(bf16[128,1152]{1,0:T(8,128)(2,1)S(1)} %get-tuple-element.35), channel_id=1, source_target_pairs={{0,48},{16,0},{32,16},{48,32},{1,49},{17,1},{33,17},{49,33},{2,50}... | collective-permute-start | bytes 884744 | tf_op jit(solution)/shard_map/ppermute | solution.py:274
  57.3 4.5 %collective-permute-done.3.refs_3_ = bf16[128,1152]{1,0:T(8,128)(2,1)S(1)} collective-permute-done((bf16[128,1152]{1,0:T(8,128)(2,1)S(1)}, bf16[128,1152]{1,0:T(8,128)(2,1)S(1)}, u32[]{:S(2)}, u32[]{:S(2)}) %collective-permute-start.3) | collective-permute-done | bytes 294944 | tf_op jit(solution)/shard_map/ppermute | solution.py:274
  61.9 4.3 %collective-permute-done.5.refs_6_ = bf16[128,1152]{1,0:T(8,128)(2,1)S(1)} collective-permute-done((bf16[128,1152]{1,0:T(8,128)(2,1)S(1)}, bf16[128,1152]{1,0:T(8,128)(2,1)S(1)}, u32[]{:S(2)}, u32[]{:S(2)}) %collective-permute-start.5) | collective-permute-done | bytes 294944 | tf_op jit(solution)/shard_map/ppermute | solution.py:274
  67.0 2.0 %collective-permute-start.7 = (bf16[32,1152]{1,0:T(8,128)(2,1)S(1)}, bf16[32,1152]{1,0:T(8,128)(2,1)S(1)}, u32[]{:S(2)}, u32[]{:S(2)}) collective-permute-start(bf16[32,1152]{1,0:T(8,128)(2,1)S(1)} %get-tuple-element.37), channel_id=1, source_target_pairs={{0,16},{16,32},{32,48},{48,0},{1,17},{17,33},{33,49},{49,1},{2,18}... | collective-permute-start | bytes 221192 | tf_op jit(solution)/shard_map/ppermute | solution.py:274
  72.3 3.5 %collective-permute-start.11 = (bf16[32,1152]{1,0:T(8,128)(2,1)S(1)}, bf16[32,1152]{1,0:T(8,128)(2,1)S(1)}, u32[]{:S(2)}, u32[]{:S(2)}) collective-permute-start(bf16[32,1152]{1,0:T(8,128)(2,1)S(1)} %get-tuple-element.42), channel_id=1, source_target_pairs={{0,128},{64,192},{128,0},{192,64},{1,129},{65,193},{129,1},{193,65... | collective-permute-start | bytes 221192 | tf_op jit(solution)/shard_map/ppermute | solution.py:274
  78.3 1.9 %collective-permute-done.12.refs_7_ = bf16[32,1152]{1,0:T(8,128)(2,1)S(1)} collective-permute-done((bf16[32,1152]{1,0:T(8,128)(2,1)S(1)}, bf16[32,1152]{1,0:T(8,128)(2,1)S(1)}, u32[]{:S(2)}, u32[]{:S(2)}) %collective-permute-start.12) | collective-permute-done | bytes 73760 | tf_op jit(solution)/shard_map/ppermute | solution.py:274
  82.7 2.4 %collective-permute-start.13 = (bf16[32,1152]{1,0:T(8,128)(2,1)S(1)}, bf16[32,1152]{1,0:T(8,128)(2,1)S(1)}, u32[]{:S(2)}, u32[]{:S(2)}) collective-permute-start(bf16[32,1152]{1,0:T(8,128)(2,1)S(1)} %get-tuple-element.44), channel_id=1, source_target_pairs={{0,64},{64,128},{128,192},{192,0},{1,65},{65,129},{129,193},{193,1... | collective-permute-start | bytes 221192 | tf_op jit(solution)/shard_map/ppermute | solution.py:274
  85.8 1.9 %collective-permute-start.20 = (bf16[32,1152]{1,0:T(8,128)(2,1)S(1)}, bf16[32,1152]{1,0:T(8,128)(2,1)S(1)}, u32[]{:S(2)}, u32[]{:S(2)}) collective-permute-start(bf16[32,1152]{1,0:T(8,128)(2,1)S(1)} %get-tuple-element.45), channel_id=1, source_target_pairs={{0,32},{16,48},{32,0},{48,16},{1,33},{17,49},{33,1},{49,17},{2,34}... | collective-permute-start | bytes 221192 | tf_op jit(solution)/shard_map/ppermute | solution.py:274
  89.5 3.1 %collective-permute-start.17 = (bf16[4,32,1152]{2,1,0:T(8,128)(2,1)S(1)}, bf16[4,32,1152]{2,1,0:T(8,128)(2,1)S(1)}, u32[]{:S(2)}, u32[]{:S(2)}) collective-permute-start(bf16[4,32,1152]{2,1,0:T(8,128)(2,1)S(1)} %pad_maximum_fusion.refs_0_), channel_id=1, source_target_pairs={{0,32},{16,48},{32,0},{48,16},{1,33},{17,49},{33,1},{49,17},{2,34}... | collective-permute-start | bytes 884744 | tf_op jit(solution)/shard_map/ppermute | solution.py:274
  96.1 3.5 %collective-permute-done.16.refs_1_ = bf16[4,32,1152]{2,1,0:T(8,128)(2,1)S(1)} collective-permute-done((bf16[4,32,1152]{2,1,0:T(8,128)(2,1)S(1)}, bf16[4,32,1152]{2,1,0:T(8,128)(2,1)S(1)}, u32[]{:S(2)}, u32[]{:S(2)}) %collective-permute-start.16) | collective-permute-done | bytes 294944 | tf_op jit(solution)/shard_map/ppermute | solution.py:274
  99.6 5.0 %collective-permute-start.24 = (bf16[4,32,1152]{2,1,0:T(8,128)(2,1)S(1)}, bf16[4,32,1152]{2,1,0:T(8,128)(2,1)S(1)}, u32[]{:S(2)}, u32[]{:S(2)}) collective-permute-start(bf16[4,32,1152]{2,1,0:T(8,128)(2,1)S(1)} %pad_maximum_fusion.1.refs_4_), channel_id=1, source_target_pairs={{0,192},{64,0},{128,64},{192,128},{1,193},{65,1},{129,65},{193,129... | collective-permute-start | bytes 884744 | tf_op jit(solution)/shard_map/ppermute | solution.py:274
  105.6 3.2 %collective-permute-done.24.refs_7_ = bf16[4,32,1152]{2,1,0:T(8,128)(2,1)S(1)} collective-permute-done((bf16[4,32,1152]{2,1,0:T(8,128)(2,1)S(1)}, bf16[4,32,1152]{2,1,0:T(8,128)(2,1)S(1)}, u32[]{:S(2)}, u32[]{:S(2)}) %collective-permute-start.24) | collective-permute-done | bytes 294944 | tf_op jit(solution)/shard_map/ppermute | solution.py:274
  111.7 10.3 %finish.1 = bf16[8,16,3584]{2,1,0:T(8,128)(2,1)} custom-call(s32[3]{0:T(128)S(1)} %pad_add_fusion.place_ref, bf16[256,2048]{1,0:T(8,128)(2,1)S(1)} %get-tuple-element.27.x_ref, bf16[4,32,1152]{2,1,0:T(8,128)(2,1)S(1)} %pad_maximum_fusion.refs_0_, bf16[4,32,1152]{2,1,0:T(8,128)(2,1)S(1)} %collective-permute-done.16.refs_1_, ...), custom_call_target="tpu_custom_call" | custom-call | tf_op jit(solution)/shard_map/finish/pallas_call | solution.py:257
  122.0 3.7 %all-to-all-start.1 = ((bf16[8,16,3584]{2,1,0:T(8,128)(2,1)}), bf16[8,16,3584]{2,1,0:T(8,128)(2,1)S(1)}, u32[]{:S(2)}, u32[]{:S(2)}) async-start(bf16[8,16,3584]{2,1,0:T(8,128)(2,1)} %finish.1), calls=%async_computation.1 | async-start | bytes 1835008 | tf_op jit(solution)/shard_map/all_to_all | solution.py:313
  126.9 1.8 %collective-permute-start.34 = (f32[1,64]{1,0:T(1,128)S(1)}, f32[1,64]{1,0:T(1,128)S(1)}, u32[]{:S(2)}, u32[]{:S(2)}) collective-permute-start(f32[1,64]{1,0:T(1,128)S(1)} %max.24), channel_id=1, source_target_pairs={{0,64},{64,128},{128,192},{192,0},{1,65},{65,129},{129,193},{193,1... | collective-permute-start | bytes 776 | tf_op jit(solution)/shard_map/ppermute | solution.py:274
  128.7 2.2 %collective-permute-done.34 = f32[1,64]{1,0:T(1,128)S(1)} collective-permute-done((f32[1,64]{1,0:T(1,128)S(1)}, f32[1,64]{1,0:T(1,128)S(1)}, u32[]{:S(2)}, u32[]{:S(2)}) %collective-permute-start.34) | collective-permute-done | bytes 288 | tf_op jit(solution)/shard_map/ppermute | solution.py:274
  130.9 2.1 %collective-permute-start.35 = (f32[1,64]{1,0:T(1,128)S(1)}, f32[1,64]{1,0:T(1,128)S(1)}, u32[]{:S(2)}, u32[]{:S(2)}) collective-permute-start(f32[1,64]{1,0:T(1,128)S(1)} %max.25), channel_id=1, source_target_pairs={{0,128},{64,192},{128,0},{192,64},{1,129},{65,193},{129,1},{193,65... | collective-permute-start | bytes 776 | tf_op jit(solution)/shard_map/ppermute | solution.py:274
  133.0 3.0 %collective-permute-done.35 = f32[1,64]{1,0:T(1,128)S(1)} collective-permute-done((f32[1,64]{1,0:T(1,128)S(1)}, f32[1,64]{1,0:T(1,128)S(1)}, u32[]{:S(2)}, u32[]{:S(2)}) %collective-permute-start.35) | collective-permute-done | bytes 288 | tf_op jit(solution)/shard_map/ppermute | solution.py:274
  135.9 4.7 %collective-permute-done.36 = f32[1,64]{1,0:T(1,128)S(1)} collective-permute-done((f32[1,64]{1,0:T(1,128)S(1)}, f32[1,64]{1,0:T(1,128)S(1)}, u32[]{:S(2)}, u32[]{:S(2)}) %collective-permute-start.36) | collective-permute-done | bytes 288 | tf_op jit(solution)/shard_map/ppermute | solution.py:274
  140.7 5.0 %collective-permute-done.37 = f32[1,64]{1,0:T(1,128)S(1)} collective-permute-done((f32[1,64]{1,0:T(1,128)S(1)}, f32[1,64]{1,0:T(1,128)S(1)}, u32[]{:S(2)}, u32[]{:S(2)}) %collective-permute-start.37) | collective-permute-done | bytes 288 | tf_op jit(solution)/shard_map/ppermute | solution.py:274
  145.7 1.8 %collective-permute-start.38 = (f32[1,64]{1,0:T(1,128)S(1)}, f32[1,64]{1,0:T(1,128)S(1)}, u32[]{:S(2)}, u32[]{:S(2)}) collective-permute-start(f32[1,64]{1,0:T(1,128)S(1)} %max.28), channel_id=1, source_target_pairs={{0,1},{1,2},{2,3},{3,4},{4,5},{5,6},{6,7},{7,0},{8,9},{9,10},{10,1... | collective-permute-start | bytes 776 | tf_op jit(solution)/shard_map/ppermute | solution.py:274
  147.6 2.9 %collective-permute-done.38 = f32[1,64]{1,0:T(1,128)S(1)} collective-permute-done((f32[1,64]{1,0:T(1,128)S(1)}, f32[1,64]{1,0:T(1,128)S(1)}, u32[]{:S(2)}, u32[]{:S(2)}) %collective-permute-start.38) | collective-permute-done | bytes 288 | tf_op jit(solution)/shard_map/ppermute | solution.py:274
  152.0 4.1 %collective-permute-done.39 = f32[1,64]{1,0:T(1,128)S(1)} collective-permute-done((f32[1,64]{1,0:T(1,128)S(1)}, f32[1,64]{1,0:T(1,128)S(1)}, u32[]{:S(2)}, u32[]{:S(2)}) %collective-permute-start.39) | collective-permute-done | bytes 288 | tf_op jit(solution)/shard_map/ppermute | solution.py:274
  156.2 5.8 %collective-permute-start.40 = (f32[1,64]{1,0:T(1,128)S(1)}, f32[1,64]{1,0:T(1,128)S(1)}, u32[]{:S(2)}, u32[]{:S(2)}) collective-permute-start(f32[1,64]{1,0:T(1,128)S(1)} %max.30), channel_id=1, source_target_pairs={{0,4},{1,5},{2,6},{3,7},{4,0},{5,1},{6,2},{7,3},{8,12},{9,13},{10,... | collective-permute-start | bytes 776 | tf_op jit(solution)/shard_map/ppermute | solution.py:274
  161.9 1.7 %collective-permute-done.40 = f32[1,64]{1,0:T(1,128)S(1)} collective-permute-done((f32[1,64]{1,0:T(1,128)S(1)}, f32[1,64]{1,0:T(1,128)S(1)}, u32[]{:S(2)}, u32[]{:S(2)}) %collective-permute-start.40) | collective-permute-done | bytes 288 | tf_op jit(solution)/shard_map/ppermute | solution.py:274
  165.3 1.7 %spread_step.1 = bf16[28,8,2048]{2,1,0:T(8,128)(2,1)} custom-call(bf16[8,16,3584]{2,1,0:T(8,128)(2,1)S(1)} %all-to-all-done.1.packed_ref), custom_call_target="tpu_custom_call" | custom-call | tf_op jit(solution)/shard_map/spread_step/pallas_call | solution.py:115
  (88 shorter events, 31.2 us)
Async XLA Ops:
  44.4 9.9 %collective-permute-start.1 = (bf16[128,1152]{1,0:T(8,128)(2,1)S(1)}, bf16[128,1152]{1,0:T(8,128)(2,1)S(1)}, u32[]{:S(2)}, u32[]{:S(2)}) collective-permute-start(bf16[128,1152]{1,0:T(8,128)(2,1)S(1)} %get-tuple-element.29), channel_id=1, source_target_pairs={{0,64},{64,128},{128,192},{192,0},{1,65},{65,129},{129,193},{193,1... | collective-permute-start | bytes 884744 | tf_op jit(solution)/shard_map/ppermute | solution.py:274
  45.9 11.4 %collective-permute-start.2 = (bf16[128,1152]{1,0:T(8,128)(2,1)S(1)}, bf16[128,1152]{1,0:T(8,128)(2,1)S(1)}, u32[]{:S(2)}, u32[]{:S(2)}) collective-permute-start(bf16[128,1152]{1,0:T(8,128)(2,1)S(1)} %get-tuple-element.30), channel_id=1, source_target_pairs={{0,128},{64,192},{128,0},{192,64},{1,129},{65,193},{129,1},{193,65... | collective-permute-start | bytes 884744 | tf_op jit(solution)/shard_map/ppermute | solution.py:274
  47.1 14.8 %collective-permute-start.3 = (bf16[128,1152]{1,0:T(8,128)(2,1)S(1)}, bf16[128,1152]{1,0:T(8,128)(2,1)S(1)}, u32[]{:S(2)}, u32[]{:S(2)}) collective-permute-start(bf16[128,1152]{1,0:T(8,128)(2,1)S(1)} %get-tuple-element.31), channel_id=1, source_target_pairs={{0,192},{64,0},{128,64},{192,128},{1,193},{65,1},{129,65},{193,129... | collective-permute-start | bytes 884744 | tf_op jit(solution)/shard_map/ppermute | solution.py:274
  49.2 12.7 %collective-permute-start.4 = (bf16[128,1152]{1,0:T(8,128)(2,1)S(1)}, bf16[128,1152]{1,0:T(8,128)(2,1)S(1)}, u32[]{:S(2)}, u32[]{:S(2)}) collective-permute-start(bf16[128,1152]{1,0:T(8,128)(2,1)S(1)} %get-tuple-element.33), channel_id=1, source_target_pairs={{0,16},{16,32},{32,48},{48,0},{1,17},{17,33},{33,49},{49,1},{2,18}... | collective-permute-start | bytes 884744 | tf_op jit(solution)/shard_map/ppermute | solution.py:274
  50.8 15.4 %collective-permute-start.5 = (bf16[128,1152]{1,0:T(8,128)(2,1)S(1)}, bf16[128,1152]{1,0:T(8,128)(2,1)S(1)}, u32[]{:S(2)}, u32[]{:S(2)}) collective-permute-start(bf16[128,1152]{1,0:T(8,128)(2,1)S(1)} %get-tuple-element.34), channel_id=1, source_target_pairs={{0,32},{16,48},{32,0},{48,16},{1,33},{17,49},{33,1},{49,17},{2,34}... | collective-permute-start | bytes 884744 | tf_op jit(solution)/shard_map/ppermute | solution.py:274
  54.3 11.9 %collective-permute-start.6 = (bf16[128,1152]{1,0:T(8,128)(2,1)S(1)}, bf16[128,1152]{1,0:T(8,128)(2,1)S(1)}, u32[]{:S(2)}, u32[]{:S(2)}) collective-permute-start(bf16[128,1152]{1,0:T(8,128)(2,1)S(1)} %get-tuple-element.35), channel_id=1, source_target_pairs={{0,48},{16,0},{32,16},{48,32},{1,49},{17,1},{33,17},{49,33},{2,50}... | collective-permute-start | bytes 884744 | tf_op jit(solution)/shard_map/ppermute | solution.py:274
  67.0 8.8 %collective-permute-start.7 = (bf16[32,1152]{1,0:T(8,128)(2,1)S(1)}, bf16[32,1152]{1,0:T(8,128)(2,1)S(1)}, u32[]{:S(2)}, u32[]{:S(2)}) collective-permute-start(bf16[32,1152]{1,0:T(8,128)(2,1)S(1)} %get-tuple-element.37), channel_id=1, source_target_pairs={{0,16},{16,32},{32,48},{48,0},{1,17},{17,33},{33,49},{49,1},{2,18}... | collective-permute-start | bytes 221192 | tf_op jit(solution)/shard_map/ppermute | solution.py:274
  69.0 6.8 %collective-permute-start.8 = (bf16[32,1152]{1,0:T(8,128)(2,1)S(1)}, bf16[32,1152]{1,0:T(8,128)(2,1)S(1)}, u32[]{:S(2)}, u32[]{:S(2)}) collective-permute-start(bf16[32,1152]{1,0:T(8,128)(2,1)S(1)} %get-tuple-element.38), channel_id=1, source_target_pairs={{0,32},{16,48},{32,0},{48,16},{1,33},{17,49},{33,1},{49,17},{2,34}... | collective-permute-start | bytes 221192 | tf_op jit(solution)/shard_map/ppermute | solution.py:274
  70.7 5.2 %collective-permute-start.9 = (bf16[32,1152]{1,0:T(8,128)(2,1)S(1)}, bf16[32,1152]{1,0:T(8,128)(2,1)S(1)}, u32[]{:S(2)}, u32[]{:S(2)}) collective-permute-start(bf16[32,1152]{1,0:T(8,128)(2,1)S(1)} %get-tuple-element.39), channel_id=1, source_target_pairs={{0,48},{16,0},{32,16},{48,32},{1,49},{17,1},{33,17},{49,33},{2,50}... | collective-permute-start | bytes 221192 | tf_op jit(solution)/shard_map/ppermute | solution.py:274
  72.3 6.0 %collective-permute-start.11 = (bf16[32,1152]{1,0:T(8,128)(2,1)S(1)}, bf16[32,1152]{1,0:T(8,128)(2,1)S(1)}, u32[]{:S(2)}, u32[]{:S(2)}) collective-permute-start(bf16[32,1152]{1,0:T(8,128)(2,1)S(1)} %get-tuple-element.42), channel_id=1, source_target_pairs={{0,128},{64,192},{128,0},{192,64},{1,129},{65,193},{129,1},{193,65... | collective-permute-start | bytes 221192 | tf_op jit(solution)/shard_map/ppermute | solution.py:274
  75.8 4.4 %collective-permute-start.12 = (bf16[32,1152]{1,0:T(8,128)(2,1)S(1)}, bf16[32,1152]{1,0:T(8,128)(2,1)S(1)}, u32[]{:S(2)}, u32[]{:S(2)}) collective-permute-start(bf16[32,1152]{1,0:T(8,128)(2,1)S(1)} %get-tuple-element.43), channel_id=1, source_target_pairs={{0,192},{64,0},{128,64},{192,128},{1,193},{65,1},{129,65},{193,129... | collective-permute-start | bytes 221192 | tf_op jit(solution)/shard_map/ppermute | solution.py:274
  80.3 7.4 %collective-permute-start.15 = (bf16[32,1152]{1,0:T(8,128)(2,1)S(1)}, bf16[32,1152]{1,0:T(8,128)(2,1)S(1)}, u32[]{:S(2)}, u32[]{:S(2)}) collective-permute-start(bf16[32,1152]{1,0:T(8,128)(2,1)S(1)} %get-tuple-element.44), channel_id=1, source_target_pairs={{0,192},{64,0},{128,64},{192,128},{1,193},{65,1},{129,65},{193,129... | collective-permute-start | bytes 221192 | tf_op jit(solution)/shard_map/ppermute | solution.py:274
  81.1 6.6 %collective-permute-start.14 = (bf16[32,1152]{1,0:T(8,128)(2,1)S(1)}, bf16[32,1152]{1,0:T(8,128)(2,1)S(1)}, u32[]{:S(2)}, u32[]{:S(2)}) collective-permute-start(bf16[32,1152]{1,0:T(8,128)(2,1)S(1)} %get-tuple-element.44), channel_id=1, source_target_pairs={{0,128},{64,192},{128,0},{192,64},{1,129},{65,193},{129,1},{193,65... | collective-permute-start | bytes 221192 | tf_op jit(solution)/shard_map/ppermute | solution.py:274
  82.7 5.0 %collective-permute-start.13 = (bf16[32,1152]{1,0:T(8,128)(2,1)S(1)}, bf16[32,1152]{1,0:T(8,128)(2,1)S(1)}, u32[]{:S(2)}, u32[]{:S(2)}) collective-permute-start(bf16[32,1152]{1,0:T(8,128)(2,1)S(1)} %get-tuple-element.44), channel_id=1, source_target_pairs={{0,64},{64,128},{128,192},{192,0},{1,65},{65,129},{129,193},{193,1... | collective-permute-start | bytes 221192 | tf_op jit(solution)/shard_map/ppermute | solution.py:274
  85.0 7.5 %collective-permute-start.21 = (bf16[32,1152]{1,0:T(8,128)(2,1)S(1)}, bf16[32,1152]{1,0:T(8,128)(2,1)S(1)}, u32[]{:S(2)}, u32[]{:S(2)}) collective-permute-start(bf16[32,1152]{1,0:T(8,128)(2,1)S(1)} %get-tuple-element.45), channel_id=1, source_target_pairs={{0,48},{16,0},{32,16},{48,32},{1,49},{17,1},{33,17},{49,33},{2,50}... | collective-permute-start | bytes 221192 | tf_op jit(solution)/shard_map/ppermute | solution.py:274
  85.8 8.1 %collective-permute-start.20 = (bf16[32,1152]{1,0:T(8,128)(2,1)S(1)}, bf16[32,1152]{1,0:T(8,128)(2,1)S(1)}, u32[]{:S(2)}, u32[]{:S(2)}) collective-permute-start(bf16[32,1152]{1,0:T(8,128)(2,1)S(1)} %get-tuple-element.45), channel_id=1, source_target_pairs={{0,32},{16,48},{32,0},{48,16},{1,33},{17,49},{33,1},{49,17},{2,34}... | collective-permute-start | bytes 221192 | tf_op jit(solution)/shard_map/ppermute | solution.py:274
  87.7 6.5 %collective-permute-start.19 = (bf16[32,1152]{1,0:T(8,128)(2,1)S(1)}, bf16[32,1152]{1,0:T(8,128)(2,1)S(1)}, u32[]{:S(2)}, u32[]{:S(2)}) collective-permute-start(bf16[32,1152]{1,0:T(8,128)(2,1)S(1)} %get-tuple-element.45), channel_id=1, source_target_pairs={{0,16},{16,32},{32,48},{48,0},{1,17},{17,33},{33,49},{49,1},{2,18}... | collective-permute-start | bytes 221192 | tf_op jit(solution)/shard_map/ppermute | solution.py:274
  87.8 11.8 %collective-permute-start.16 = (bf16[4,32,1152]{2,1,0:T(8,128)(2,1)S(1)}, bf16[4,32,1152]{2,1,0:T(8,128)(2,1)S(1)}, u32[]{:S(2)}, u32[]{:S(2)}) collective-permute-start(bf16[4,32,1152]{2,1,0:T(8,128)(2,1)S(1)} %pad_maximum_fusion.refs_0_), channel_id=1, source_target_pairs={{0,16},{16,32},{32,48},{48,0},{1,17},{17,33},{33,49},{49,1},{2,18}... | collective-permute-start | bytes 884744 | tf_op jit(solution)/shard_map/ppermute | solution.py:274
  89.5 15.1 %collective-permute-start.17 = (bf16[4,32,1152]{2,1,0:T(8,128)(2,1)S(1)}, bf16[4,32,1152]{2,1,0:T(8,128)(2,1)S(1)}, u32[]{:S(2)}, u32[]{:S(2)}) collective-permute-start(bf16[4,32,1152]{2,1,0:T(8,128)(2,1)S(1)} %pad_maximum_fusion.refs_0_), channel_id=1, source_target_pairs={{0,32},{16,48},{32,0},{48,16},{1,33},{17,49},{33,1},{49,17},{2,34}... | collective-permute-start | bytes 884744 | tf_op jit(solution)/shard_map/ppermute | solution.py:274
  92.5 12.0 %collective-permute-start.18 = (bf16[4,32,1152]{2,1,0:T(8,128)(2,1)S(1)}, bf16[4,32,1152]{2,1,0:T(8,128)(2,1)S(1)}, u32[]{:S(2)}, u32[]{:S(2)}) collective-permute-start(bf16[4,32,1152]{2,1,0:T(8,128)(2,1)S(1)} %pad_maximum_fusion.refs_0_), channel_id=1, source_target_pairs={{0,48},{16,0},{32,16},{48,32},{1,49},{17,1},{33,17},{49,33},{2,50}... | collective-permute-start | bytes 884744 | tf_op jit(solution)/shard_map/ppermute | solution.py:274
  94.2 10.9 %collective-permute-start.22 = (bf16[4,32,1152]{2,1,0:T(8,128)(2,1)S(1)}, bf16[4,32,1152]{2,1,0:T(8,128)(2,1)S(1)}, u32[]{:S(2)}, u32[]{:S(2)}) collective-permute-start(bf16[4,32,1152]{2,1,0:T(8,128)(2,1)S(1)} %pad_maximum_fusion.1.refs_4_), channel_id=1, source_target_pairs={{0,64},{64,128},{128,192},{192,0},{1,65},{65,129},{129,193},{193,1... | collective-permute-start | bytes 884744 | tf_op jit(solution)/shard_map/ppermute | solution.py:274
  95.4 9.7 %collective-permute-start.23 = (bf16[4,32,1152]{2,1,0:T(8,128)(2,1)S(1)}, bf16[4,32,1152]{2,1,0:T(8,128)(2,1)S(1)}, u32[]{:S(2)}, u32[]{:S(2)}) collective-permute-start(bf16[4,32,1152]{2,1,0:T(8,128)(2,1)S(1)} %pad_maximum_fusion.1.refs_4_), channel_id=1, source_target_pairs={{0,128},{64,192},{128,0},{192,64},{1,129},{65,193},{129,1},{193,65... | collective-permute-start | bytes 884744 | tf_op jit(solution)/shard_map/ppermute | solution.py:274
  99.6 9.2 %collective-permute-start.24 = (bf16[4,32,1152]{2,1,0:T(8,128)(2,1)S(1)}, bf16[4,32,1152]{2,1,0:T(8,128)(2,1)S(1)}, u32[]{:S(2)}, u32[]{:S(2)}) collective-permute-start(bf16[4,32,1152]{2,1,0:T(8,128)(2,1)S(1)} %pad_maximum_fusion.1.refs_4_), channel_id=1, source_target_pairs={{0,192},{64,0},{128,64},{192,128},{1,193},{65,1},{129,65},{193,129... | collective-permute-start | bytes 884744 | tf_op jit(solution)/shard_map/ppermute | solution.py:274
  104.6 4.7 %collective-permute-start.29 = (bf16[4,32,1152]{2,1,0:T(8,128)(2,1)S(1)}, bf16[4,32,1152]{2,1,0:T(8,128)(2,1)S(1)}, u32[]{:S(2)}, u32[]{:S(2)}) collective-permute-start(bf16[4,32,1152]{2,1,0:T(8,128)(2,1)S(1)} %pad_maximum_fusion.1.refs_4_), channel_id=1, source_target_pairs={{0,8},{8,0},{1,9},{9,1},{2,10},{10,2},{3,11},{11,3},{4,12},{12,4},... | collective-permute-start | bytes 884744 | tf_op jit(solution)/shard_map/ppermute | solution.py:278
  105.2 4.7 %collective-permute-start.27 = (bf16[4,32,1152]{2,1,0:T(8,128)(2,1)S(1)}, bf16[4,32,1152]{2,1,0:T(8,128)(2,1)S(1)}, u32[]{:S(2)}, u32[]{:S(2)}) collective-permute-start(bf16[4,32,1152]{2,1,0:T(8,128)(2,1)S(1)} %collective-permute-done.17.refs_2_), channel_id=1, source_target_pairs={{0,8},{8,0},{1,9},{9,1},{2,10},{10,2},{3,11},{11,3},{4,12},{12,4},... | collective-permute-start | bytes 884744 | tf_op jit(solution)/shard_map/ppermute | solution.py:278
  122.0 43.3 %all-to-all-start.1 = ((bf16[8,16,3584]{2,1,0:T(8,128)(2,1)}), bf16[8,16,3584]{2,1,0:T(8,128)(2,1)S(1)}, u32[]{:S(2)}, u32[]{:S(2)}) async-start(bf16[8,16,3584]{2,1,0:T(8,128)(2,1)} %finish.1), calls=%async_computation.1 | async-start | bytes 1835008 | tf_op jit(solution)/shard_map/all_to_all | solution.py:313
  130.9 5.0 %collective-permute-start.35 = (f32[1,64]{1,0:T(1,128)S(1)}, f32[1,64]{1,0:T(1,128)S(1)}, u32[]{:S(2)}, u32[]{:S(2)}) collective-permute-start(f32[1,64]{1,0:T(1,128)S(1)} %max.25), channel_id=1, source_target_pairs={{0,128},{64,192},{128,0},{192,64},{1,129},{65,193},{129,1},{193,65... | collective-permute-start | bytes 776 | tf_op jit(solution)/shard_map/ppermute | solution.py:274
  135.9 4.8 %collective-permute-start.36 = (f32[1,64]{1,0:T(1,128)S(1)}, f32[1,64]{1,0:T(1,128)S(1)}, u32[]{:S(2)}, u32[]{:S(2)}) collective-permute-start(f32[1,64]{1,0:T(1,128)S(1)} %max.26), channel_id=1, source_target_pairs={{0,16},{16,32},{32,48},{48,0},{1,17},{17,33},{33,49},{49,1},{2,18}... | collective-permute-start | bytes 776 | tf_op jit(solution)/shard_map/ppermute | solution.py:274
  140.7 5.0 %collective-permute-start.37 = (f32[1,64]{1,0:T(1,128)S(1)}, f32[1,64]{1,0:T(1,128)S(1)}, u32[]{:S(2)}, u32[]{:S(2)}) collective-permute-start(f32[1,64]{1,0:T(1,128)S(1)} %max.27), channel_id=1, source_target_pairs={{0,32},{16,48},{32,0},{48,16},{1,33},{17,49},{33,1},{49,17},{2,34}... | collective-permute-start | bytes 776 | tf_op jit(solution)/shard_map/ppermute | solution.py:274
  145.7 4.8 %collective-permute-start.38 = (f32[1,64]{1,0:T(1,128)S(1)}, f32[1,64]{1,0:T(1,128)S(1)}, u32[]{:S(2)}, u32[]{:S(2)}) collective-permute-start(f32[1,64]{1,0:T(1,128)S(1)} %max.28), channel_id=1, source_target_pairs={{0,1},{1,2},{2,3},{3,4},{4,5},{5,6},{6,7},{7,0},{8,9},{9,10},{10,1... | collective-permute-start | bytes 776 | tf_op jit(solution)/shard_map/ppermute | solution.py:274
  150.5 5.7 %collective-permute-start.39 = (f32[1,64]{1,0:T(1,128)S(1)}, f32[1,64]{1,0:T(1,128)S(1)}, u32[]{:S(2)}, u32[]{:S(2)}) collective-permute-start(f32[1,64]{1,0:T(1,128)S(1)} %max.29), channel_id=1, source_target_pairs={{0,2},{1,3},{2,4},{3,5},{4,6},{5,7},{6,0},{7,1},{8,10},{9,11},{10,... | collective-permute-start | bytes 776 | tf_op jit(solution)/shard_map/ppermute | solution.py:274
  156.2 7.4 %collective-permute-start.40 = (f32[1,64]{1,0:T(1,128)S(1)}, f32[1,64]{1,0:T(1,128)S(1)}, u32[]{:S(2)}, u32[]{:S(2)}) collective-permute-start(f32[1,64]{1,0:T(1,128)S(1)} %max.30), channel_id=1, source_target_pairs={{0,4},{1,5},{2,6},{3,7},{4,0},{5,1},{6,2},{7,3},{8,12},{9,13},{10,... | collective-permute-start | bytes 776 | tf_op jit(solution)/shard_map/ppermute | solution.py:274
  (15 other events, 119.4 us)
where the time goes:
time: 169 us; the launch traced here: 167 us
  starting transfers between devices  60.5 us (36%)
  waiting for transfers between devices  49.7 us (29%)
  blocking collectives  34.2 us (20%)
  Pallas kernels  17.4 us (10%)
  local copies, waits for them, and re-layouts  3.04 us (2%)
    ppermute x32, starting transfers between devices, shift(): lax.ppermute(value, axis, [(i, (i + by) % size) for i in range(size)])  54.8 us
    ppermute x32, waiting for transfers between devices, shift(): lax.ppermute(value, axis, [(i, (i + by) % size) for i in range(size)])  45.5 us
    all_to_all x1, blocking collectives, body(): lax.all_to_all(direction, 'z', split_axis=0, concat_axis=0, tiled=True)  34.2 us
    pallas_call x1, Pallas kernels, finish(): pl.pallas_call(step_kernel, out_shape=jax.ShapeDtypeStruct((NZ, 16, PACKE...  10.3 us
    ppermute x9, waiting for transfers between devices, swap_cores(): return lax.ppermute(value, 'c', [(0, 1), (1, 0)])  4.21 us
    all_to_all x1, starting transfers between devices, body(): step = lax.all_to_all(step, 'z', split_axis=0, concat_axis=0, tiled=True)  3.68 us
  transfers between devices with their start and end apart: 42, of which 22 were waited for; matrix products, arithmetic and copies ran while one was open for 1% of the time, Pallas kernels for 0%

commit v1 on v0

--- a/solution.py
+++ b/solution.py
@@ -20,6 +20,7 @@
 rms_match = 0.2
 
 NX, NY, NC, NZ = 4, 4, 2, 8
+PLANE = ("x", "y", "c")
 BLK = 128
 NB = FF // BLK
 HALF = FF // 2
@@ -29,7 +30,7 @@
 CUT = 512
 TAIL = 384
 PACKED = FF + (FF // CUT) * TAIL
-SHARE = BLK // 4
+QUARTER = 2 * BLK
 
 MASS = pl.BlockSpec(memory_space=pltpu.VMEM)
 SCALARS = pl.BlockSpec(memory_space=pltpu.SMEM)
@@ -74,11 +75,10 @@
     return pl.ds(pl.multiple_of(FF + n * TAIL, BLK), TAIL)
 
 
-def direction_kernel(grads_ref, momentum_ref, new_ref, out_ref):
+def direction_kernel(grads_ref, momentum_ref, out_ref):
     n = pl.program_id(0)
     grads = grads_ref[...].astype(jnp.float32)
     new = decay_rate * momentum_ref[...] + grads
-    new_ref[...] = new
     direction = grads + decay_rate * new
     rows, mats, columns = direction.shape
     direction = jnp.concatenate([direction, jnp.zeros((PADROWS - rows, mats, columns), jnp.float32)], axis=0)
@@ -93,13 +93,10 @@
     return pl.pallas_call(
         direction_kernel,
         grid=(FF // CUT,),
-        out_shape=(
-            jax.ShapeDtypeStruct(grads.shape, jnp.float32),
-            jax.ShapeDtypeStruct((mats, 16, PACKED), jnp.bfloat16),
-        ),
+        out_shape=jax.ShapeDtypeStruct((mats, 16, PACKED), jnp.bfloat16),
         in_specs=[cut, cut],
-        out_specs=(cut, pl.BlockSpec((mats, 16, PACKED), lambda n: (0, 0, 0))),
-        compiler_params=room(24),
+        out_specs=pl.BlockSpec((mats, 16, PACKED), lambda n: (0, 0, 0)),
+        compiler_params=room(60),
         name="find_direction",
     )(grads, momentum)
 
@@ -124,8 +121,8 @@
 
 
 def gram_kernel(place_ref, mine_ref, other_ref, *refs):
-    shares, (x_ref, rows_ref, band_ref) = refs[:8], refs[8:]
-    x, y, core = place_ref[0], place_ref[1], place_ref[2]
+    shares, (x_ref, rows_ref, band_ref) = refs[:4], refs[4:]
+    along, core = place_ref[0], place_ref[2]
     for n in range(FF // CUT):
         source = (n + 2 * core) % 4
         columns = pl.ds(n * CUT, CUT)
@@ -135,28 +132,31 @@
             rows_ref[pl.ds(half * KROWS, KROWS), columns] = rows
             if half == 0:
                 x_ref[:, columns] = rows
-    for pair in range(NB // 4):
-        left = rows_ref[:, pl.ds(pair * 2 * BLK, 2 * BLK)]
-        right = rows_ref[:, pl.ds(pair * 2 * BLK, BAND + BLK)]
+    for q in range(4):
+        left = rows_ref[:, pl.ds(q * QUARTER, QUARTER)]
+        right = rows_ref[:, pl.ds(q * QUARTER, BAND + BLK)]
         product = lax.dot_general(
             left, right, (((0,), (0,)), ((), ())), preferred_element_type=jnp.float32
         ).astype(jnp.bfloat16)
         for sub in range(2):
-            band_ref[pl.ds((pair * 2 + sub) * BLK, BLK), :] = product[
+            band_ref[pl.ds(q * QUARTER + sub * BLK, BLK), :] = product[
                 sub * BLK : (sub + 1) * BLK, sub * BLK : sub * BLK + BAND
             ]
     for d in range(4):
-        shares[d][...] = band_ref[pl.ds(pl.multiple_of(((x + d) % 4) * BLK, BLK), BLK), :]
-        shares[4 + d][...] = band_ref[pl.ds(pl.multiple_of((4 + (y + d) % 4) * BLK, BLK), BLK), :]
+        shares[d][...] = band_ref[quarter_rows(along + d), :]
+
+
+def quarter_rows(q, start=0):
+    return pl.ds(pl.multiple_of(start + (q % 4) * QUARTER, QUARTER), QUARTER)
 
 
 def gram_band(place, mine, other):
     return pl.pallas_call(
         gram_kernel,
-        out_shape=[jax.ShapeDtypeStruct((BLK, BAND), jnp.bfloat16)] * 8
+        out_shape=[jax.ShapeDtypeStruct((QUARTER, BAND), jnp.bfloat16)] * 4
         + [jax.ShapeDtypeStruct((KROWS, FF), jnp.bfloat16)],
         in_specs=[SCALARS, MASS, MASS],
-        out_specs=[MASS] * 9,
+        out_specs=[MASS] * 5,
         scratch_shapes=[
             pltpu.VMEM((2 * KROWS, FF), jnp.bfloat16),
             pltpu.VMEM((HALF, BAND), jnp.bfloat16),
@@ -166,59 +166,58 @@
     )(place, mine, other)
 
 
-def partial_kernel(place_ref, *refs):
-    parts, outs = refs[:8], refs[8:]
-    for kind in range(2):
-        here = place_ref[1 - kind]
-        for d in range(4):
-            rows = pl.ds(pl.multiple_of(((here + d) % 4) * SHARE, SHARE), SHARE)
-            total = sum(part[rows, :].astype(jnp.float32) for part in parts[4 * kind : 4 * kind + 4])
-            outs[4 * kind + d][...] = total.astype(jnp.bfloat16)
-
-
-def partial_sums(place, parts):
-    return pl.pallas_call(
-        partial_kernel,
-        out_shape=[jax.ShapeDtypeStruct((SHARE, BAND), jnp.bfloat16)] * 8,
-        in_specs=[SCALARS] + [MASS] * 8,
-        out_specs=[MASS] * 8,
-        compiler_params=room(16),
-        name="partial_sums",
-    )(place, *parts)
-
-
-def total_kernel(*refs):
-    parts, outs = refs[:8], refs[8:]
-    for kind in range(2):
-        total = sum(part[...].astype(jnp.float32) for part in parts[4 * kind : 4 * kind + 4])
-        outs[kind][...] = total.astype(jnp.bfloat16)
-
-
-def total_sums(parts):
-    return pl.pallas_call(
-        total_kernel,
-        out_shape=[jax.ShapeDtypeStruct((SHARE, BAND), jnp.bfloat16)] * 2,
-        in_specs=[MASS] * 8,
+def quarter_kernel(*refs):
+    parts, outs = refs[:4], refs[4:]
+    for half in range(2):
+        rows = pl.ds(half * BLK, BLK)
+        total = sum(part[rows, :].astype(jnp.float32) for part in parts)
+        outs[half][...] = total.astype(jnp.bfloat16)
+
+
+def sum_quarter(parts):
+    return pl.pallas_call(
+        quarter_kernel,
+        out_shape=[jax.ShapeDtypeStruct((BLK, BAND), jnp.bfloat16)] * 2,
+        in_specs=[MASS] * 4,
         out_specs=[MASS] * 2,
         compiler_params=room(16),
-        name="total_sums",
+        name="sum_quarter",
     )(*parts)
 
 
+def pair_kernel(*refs):
+    mine, came, outs = refs[:2], refs[2:4], refs[4:]
+    for half in range(2):
+        total = mine[half][...].astype(jnp.float32) + came[half][...].astype(jnp.float32)
+        if len(outs) == 2:
+            outs[half][...] = total.astype(jnp.bfloat16)
+        else:
+            outs[0][pl.ds(half * BLK, BLK), :] = total.astype(jnp.bfloat16)
+
+
+def add_pairs(mine, came, joined):
+    if joined:
+        shapes = [jax.ShapeDtypeStruct((QUARTER, BAND), jnp.bfloat16)]
+    else:
+        shapes = [jax.ShapeDtypeStruct((BLK, BAND), jnp.bfloat16)] * 2
+    return pl.pallas_call(
+        pair_kernel,
+        out_shape=shapes,
+        in_specs=[MASS] * 4,
+        out_specs=[MASS] * len(shapes),
+        compiler_params=room(16),
+        name="add_pairs",
+    )(*mine, *came)
+
+
 def step_kernel(place_ref, x_ref, *refs):
-    pieces = refs[:16]
-    out_ref, band_ref, gram_ref, first_ref, round_ref = refs[16:]
-    x, y, core = place_ref[0], place_ref[1], place_ref[2]
+    pieces = refs[:8]
+    out_ref, band_ref, gram_ref, first_ref, round_ref = refs[8:]
+    core = place_ref[2]
     for side in range(2):
-        for kind in range(2):
-            for outer in range(4):
-                piece = pieces[side * 8 + kind * 4 + outer]
-                for inner in range(4):
-                    dx, dy = (inner, outer) if kind == 0 else (outer, inner)
-                    sx, sy = (x + (4 - dx)) % 4, (y + (4 - dy)) % 4
-                    share = sx * 4 + sy if kind == 0 else 16 + sy * 4 + sx
-                    row = pl.multiple_of(side * HALF + share * SHARE, SHARE)
-                    band_ref[pl.ds(row, SHARE), :] = piece[inner]
+        for d in range(4):
+            rows = quarter_rows(place_ref[side] + (4 - d), side * HALF)
+            band_ref[rows, :] = pieces[side * 4 + d][...]
     for i in range(NB):
         block = band_ref[pl.ds(i * BLK, BLK), :]
         turned = block[:, BLK : BAND - BLK].T
@@ -257,7 +256,7 @@
     return pl.pallas_call(
         step_kernel,
         out_shape=jax.ShapeDtypeStruct((NZ, 16, PACKED), jnp.bfloat16),
-        in_specs=[SCALARS] + [MASS] * 17,
+        in_specs=[SCALARS] + [MASS] * 9,
         out_specs=MASS,
         scratch_shapes=[
             pltpu.VMEM((FF, BAND), jnp.bfloat16),
@@ -270,50 +269,80 @@
     )(place, mine, *pieces)
 
 
-def shift(value, axis, by, size):
-    return lax.ppermute(value, axis, [(i, (i + by) % size) for i in range(size)])
+def place_of(x, y, core):
+    return (x * NY + y) * NC + core
+
+
+def permutation(step):
+    pairs = []
+    for x in range(NX):
+        for y in range(NY):
+            for core in range(NC):
+                mine = (x, y) if core == 0 else (y, x)
+                to = step(*mine)
+                to = to if core == 0 else to[::-1]
+                pairs.append((place_of(x, y, core), place_of(*to, core)))
+    return pairs
+
+
+def send_along(value, by):
+    return lax.ppermute(value, PLANE, permutation(lambda along, across: ((along + by) % 4, across)))
+
+
+LINKS = ((1, 0, 3, 2), (3, 2, 1, 0))
+
+
+def trade_across(values, first):
+    links = (LINKS[first], LINKS[1 - first])
+    return [
+        lax.ppermute(value, PLANE, permutation(lambda along, across, link=link: (along, link[across])))
+        for value, link in zip(values, links)
+    ]
+
+
+def collect(own, sends):
+    came = {d: send_along(sends(d), d) for d in (2, 1, 3)}
+    return [own, came[1], came[2], came[3]]
 
 
 def swap_cores(value):
     return lax.ppermute(value, "c", [(0, 1), (1, 0)])
 
 
-def spread(value, axis):
-    return [value] + [shift(value, axis, d, 4) for d in range(1, 4)]
-
-
-def largest(value):
-    for axis, size in (("c", NC), ("x", NX), ("y", NY), ("z", NZ)):
-        by = 1
-        while by < size:
-            value = jnp.maximum(value, shift(value, axis, by, size))
-            by *= 2
-    return value
+def largest(value, axis, by, size):
+    return jnp.maximum(value, lax.ppermute(value, axis, [(i, (i + by) % size) for i in range(size)]))
 
 
 def body(grads, momentum, max_logits, q_weight, k_weight):
     x, y, core = lax.axis_index("x"), lax.axis_index("y"), lax.axis_index("c")
-    place = jnp.stack([x, y, core]).astype(jnp.int32)
+    place = jnp.stack([jnp.where(core == 0, x, y), jnp.where(core == 0, y, x), core]).astype(jnp.int32)
     rows = grads.shape[1]
-    new_momentum, direction = find_direction(jnp.swapaxes(grads, 0, 1), jnp.swapaxes(momentum, 0, 1))
-    new_momentum = jnp.swapaxes(new_momentum, 0, 1)
+    direction = find_direction(jnp.swapaxes(grads, 0, 1), jnp.swapaxes(momentum, 0, 1))
+    direction, peak, grads, momentum = lax.optimization_barrier((direction, max_logits, grads, momentum))
     owned = lax.all_to_all(direction, "z", split_axis=0, concat_axis=0, tiled=True)
+    new_momentum = decay_rate * momentum + grads.astype(jnp.float32)
+    for axis, by, size in (("c", 1, NC), ("x", 1, NX), ("x", 2, NX), ("y", 1, NY), ("y", 2, NY)):
+        peak = largest(peak, axis, by, size)
+    owned, peak, new_momentum = lax.optimization_barrier((owned, peak, new_momentum))
     *shares, mine = gram_band(place, owned, swap_cores(owned))
-    parts = [shares[0]] + [shift(shares[d], "x", d, 4) for d in range(1, 4)]
-    parts += [shares[4]] + [shift(shares[4 + d], "y", d, 4) for d in range(1, 4)]
-    shares = partial_sums(place, parts)
-    parts = [shares[0]] + [shift(shares[d], "y", d, 4) for d in range(1, 4)]
-    parts += [shares[4]] + [shift(shares[4 + d], "x", d, 4) for d in range(1, 4)]
-    a, b = total_sums(parts)
-    a = jnp.stack(spread(a, "x"))
-    b = jnp.stack(spread(b, "y"))
-    own = spread(a, "y") + spread(b, "x")
-    other = [swap_cores(piece) for piece in own]
-    step = finish(place, mine, own + other)
+    shares[0], peak = lax.optimization_barrier((shares[0], peak))
+    parts = collect(shares[0], lambda d: shares[d])
+    for by in (1, 2):
+        peak = largest(peak, "z", by, NZ)
+    parts[0], peak = lax.optimization_barrier((parts[0], peak))
+    held = sum_quarter(parts)
+    held = add_pairs(held, trade_across(held, 0), False)
+    held, = add_pairs(held, trade_across(held, 1), True)
+    held, peak = lax.optimization_barrier((held, peak))
+    pieces = collect(held, lambda d: held)
+    peak = largest(peak, "z", 4, NZ)
+    pieces[0], pieces[2], peak = lax.optimization_barrier((pieces[0], pieces[2], peak))
+    other = [swap_cores(piece) for piece in pieces]
+    step = finish(place, mine, pieces + other)
+    step, peak, q_weight, k_weight = lax.optimization_barrier((step, peak, q_weight, k_weight))
     step = lax.all_to_all(step, "z", split_axis=0, concat_axis=0, tiled=True)
-    step = jnp.swapaxes(spread_step(step, rows), 0, 1)
-
-    peak = largest(max_logits)[0]
+    peak = peak[0]
+
     gamma = jnp.minimum(1.0, clip_limit / peak)
     root = jnp.sqrt(gamma)
     local_heads = k_weight.shape[1] // NOPE
@@ -331,6 +360,8 @@
     q_clipped = (q_view * q_factor[None]).astype(jnp.bfloat16).reshape(q_weight.shape)
     k_view = k_weight.reshape(k_weight.shape[0], local_heads, NOPE).astype(jnp.float32)
     k_clipped = (k_view * root_mine[None, :, None]).astype(jnp.bfloat16).reshape(k_weight.shape)
+    step, q_clipped, k_clipped = lax.optimization_barrier((step, q_clipped, k_clipped))
+    step = jnp.swapaxes(spread_step(step, rows), 0, 1)
     return (new_momentum, step, q_clipped, k_clipped)
 
 

time: 169 us -> 146 us (0.86); the launches traced: 167 us -> 146 us
  waiting for transfers between devices: 49.7 us -> 86.4 us
  blocking collectives: 34.2 us -> 0 us
  starting transfers between devices: 60.5 us -> 35.8 us
  local copies, waits for them, and re-layouts: 3.04 us -> 0.38 us
  other arithmetic: 1.53 us -> 4.08 us
    all_to_all x1 -> x0, blocking collectives: 34.2 us -> none  [body(): lax.all_to_all(direction, 'z', split_axis=0, concat_axis=0, tiled=True)]
    ppermute x32 -> x18, starting transfers between devices: 54.8 us -> 23 us  [the longest x6 8.46 us: send_along(): lax.ppermute(value, PLANE, permutation(lambda along, across: ((along + by...]
    all_to_all x1, waiting for transfers between devices: 0.01 us -> 24.7 us  [body(): step = lax.all_to_all(step, 'z', split_axis=0, concat_axis=0, tiled=True)]
    all_to_all x0 -> x1, starting transfers between devices: none -> 8.6 us  [body(): lax.all_to_all(direction, 'z', split_axis=0, concat_axis=0, tiled=True)]
    all_to_all x0 -> x1, waiting for transfers between devices: none -> 6.31 us  [body(): lax.all_to_all(direction, 'z', split_axis=0, concat_axis=0, tiled=True)]
    ppermute x32 -> x18, waiting for transfers between devices: 45.5 us -> 50.4 us  [the longest x8 26.4 us: largest(): lax.ppermute(value, axis, [(i, (i + by) % size) for i in range(size)])]
    unnamed x10 -> x8, local copies, waits for them, and re-layouts: 2.68 us -> 0.02 us
    add x0 -> x1, other arithmetic: none -> 2.65 us  [body(): new_momentum = decay_rate * momentum + grads.astype(jnp.float32)]
  transfers between devices with their start and end apart: 42 -> 25, of which waited for: 22 -> 22; matrix products, arithmetic and copies ran while one was open for 1% -> 3% of each run, Pallas kernels for 0% -> 0%
where the time goes in v1:
time: 146 us
  waiting for transfers between devices  86.4 us (59%)
  starting transfers between devices  35.8 us (25%)
  Pallas kernels  18.7 us (13%)
  other arithmetic  4.08 us (3%)
    ppermute x8, waiting for transfers between devices, largest(): lax.ppermute(value, axis, [(i, (i + by) % size) for i in range(size)])  26.4 us
    all_to_all x1, waiting for transfers between devices, body(): step = lax.all_to_all(step, 'z', split_axis=0, concat_axis=0, tiled=True)  24.7 us
    ppermute x4, waiting for transfers between devices, trade_across(): lax.ppermute(value, PLANE, permutation(lambda along, across, link=link: (...  13.7 us
    ppermute x6, waiting for transfers between devices, send_along(): lax.ppermute(value, PLANE, permutation(lambda along, across: ((along + by...  10.4 us
    pallas_call x1, Pallas kernels, finish(): pl.pallas_call(step_kernel, out_shape=jax.ShapeDtypeStruct((NZ, 16, PACKE...  10.3 us
    all_to_all x1, starting transfers between devices, body(): lax.all_to_all(direction, 'z', split_axis=0, concat_axis=0, tiled=True)  8.6 us
    ppermute x6, starting transfers between devices, send_along(): lax.ppermute(value, PLANE, permutation(lambda along, across: ((along + by...  8.46 us
    ppermute x8, starting transfers between devices, largest(): lax.ppermute(value, axis, [(i, (i + by) % size) for i in range(size)])  8.43 us
  transfers between devices with their start and end apart: 25, of which 22 were waited for; matrix products, arithmetic and copies ran while one was open for 3% of the time, Pallas kernels for 0%

profile of v1, /device:TPU:2, one launch (start us, length us, event | category | flops | bytes accessed | tf_op | source)
XLA Modules:
  0.0 146.1 jit_solution(10850950300803179483)
XLA Ops:
  0.6 3.8 %find_direction.1 = bf16[8,16,3584]{2,1,0:T(8,128)(2,1)} custom-call(bf16[28,8,2048]{2,1,0:T(8,128)(2,1)} %bitcast.13, f32[28,8,2048]{2,1,0:T(8,128)} %bitcast.12), custom_call_target="tpu_custom_call" | custom-call | tf_op jit(solution)/shard_map/find_direction/pallas_call | solution.py:93
  4.5 8.6 %all-to-all-start = ((bf16[8,16,3584]{2,1,0:T(8,128)(2,1)}), bf16[8,16,3584]{2,1,0:T(8,128)(2,1)S(1)}, u32[]{:S(2)}, u32[]{:S(2)}) async-start(bf16[8,16,3584]{2,1,0:T(8,128)(2,1)} %find_direction.1), calls=%async_computation | async-start | bytes 1835008 | tf_op jit(solution)/shard_map/all_to_all | solution.py:322
  14.3 1.5 %collective-permute-start.1 = (f32[1,64]{1,0:T(1,128)S(1)}, f32[1,64]{1,0:T(1,128)S(1)}, u32[]{:S(2)}, u32[]{:S(2)}) collective-permute-start(f32[1,64]{1,0:T(1,128)S(1)} %max.24), channel_id=1, source_target_pairs={{0,64},{64,128},{128,192},{192,0},{1,65},{65,129},{129,193},{193,1... | collective-permute-start | bytes 776 | tf_op jit(solution)/shard_map/ppermute | solution.py:313
  15.8 2.0 %collective-permute-done.1 = f32[1,64]{1,0:T(1,128)S(1)} collective-permute-done((f32[1,64]{1,0:T(1,128)S(1)}, f32[1,64]{1,0:T(1,128)S(1)}, u32[]{:S(2)}, u32[]{:S(2)}) %collective-permute-start.1) | collective-permute-done | bytes 288 | tf_op jit(solution)/shard_map/ppermute | solution.py:313
  17.8 2.1 %collective-permute-start.2 = (f32[1,64]{1,0:T(1,128)S(1)}, f32[1,64]{1,0:T(1,128)S(1)}, u32[]{:S(2)}, u32[]{:S(2)}) collective-permute-start(f32[1,64]{1,0:T(1,128)S(1)} %max.25), channel_id=1, source_target_pairs={{0,128},{64,192},{128,0},{192,64},{1,129},{65,193},{129,1},{193,65... | collective-permute-start | bytes 776 | tf_op jit(solution)/shard_map/ppermute | solution.py:313
  20.0 2.9 %collective-permute-done.2 = f32[1,64]{1,0:T(1,128)S(1)} collective-permute-done((f32[1,64]{1,0:T(1,128)S(1)}, f32[1,64]{1,0:T(1,128)S(1)}, u32[]{:S(2)}, u32[]{:S(2)}) %collective-permute-start.2) | collective-permute-done | bytes 288 | tf_op jit(solution)/shard_map/ppermute | solution.py:313
  22.9 1.6 %collective-permute-start.3 = (f32[1,64]{1,0:T(1,128)S(1)}, f32[1,64]{1,0:T(1,128)S(1)}, u32[]{:S(2)}, u32[]{:S(2)}) collective-permute-start(f32[1,64]{1,0:T(1,128)S(1)} %max.26), channel_id=1, source_target_pairs={{0,16},{16,32},{32,48},{48,0},{1,17},{17,33},{33,49},{49,1},{2,18}... | collective-permute-start | bytes 776 | tf_op jit(solution)/shard_map/ppermute | solution.py:313
  24.5 3.2 %collective-permute-done.3 = f32[1,64]{1,0:T(1,128)S(1)} collective-permute-done((f32[1,64]{1,0:T(1,128)S(1)}, f32[1,64]{1,0:T(1,128)S(1)}, u32[]{:S(2)}, u32[]{:S(2)}) %collective-permute-start.3) | collective-permute-done | bytes 288 | tf_op jit(solution)/shard_map/ppermute | solution.py:313
  27.6 2.0 %collective-permute-start.4 = (f32[1,64]{1,0:T(1,128)S(1)}, f32[1,64]{1,0:T(1,128)S(1)}, u32[]{:S(2)}, u32[]{:S(2)}) collective-permute-start(f32[1,64]{1,0:T(1,128)S(1)} %max.27), channel_id=1, source_target_pairs={{0,32},{16,48},{32,0},{48,16},{1,33},{17,49},{33,1},{49,17},{2,34}... | collective-permute-start | bytes 776 | tf_op jit(solution)/shard_map/ppermute | solution.py:313
  29.6 2.6 %convert_add_fusion = f32[8,28,2048]{2,0,1:T(8,128)} fusion(bf16[8,28,2048]{2,0,1:T(8,128)(2,1)} %param.5, f32[8,28,2048]{2,0,1:T(8,128)S(1)} %copy-done), kind=kLoop, calls=%fused_computation | loop fusion | flops 1376256 | bytes 4587520 | tf_op jit(solution)/shard_map/add | solution.py:323
  32.7 6.3 %all-to-all-done.mine_ref = bf16[8,16,3584]{2,1,0:T(8,128)(2,1)S(1)} async-done(((bf16[8,16,3584]{2,1,0:T(8,128)(2,1)}), bf16[8,16,3584]{2,1,0:T(8,128)(2,1)S(1)}, u32[]{:S(2)}, u32[]{:S(2)}) %all-to-all-start) | async-done | bytes 917536 | tf_op jit(solution)/shard_map/all_to_all | solution.py:322
  39.1 2.4 %collective-permute-done.5.other_ref = bf16[8,16,3584]{2,1,0:T(8,128)(2,1)S(1)} collective-permute-done((bf16[8,16,3584]{2,1,0:T(8,128)(2,1)S(1)}, bf16[8,16,3584]{2,1,0:T(8,128)(2,1)S(1)}, u32[]{:S(2)}, u32[]{:S(2)}) %collective-permute-start.5) | collective-permute-done | bytes 917536 | tf_op jit(solution)/shard_map/ppermute | solution.py:309
  41.5 2.3 %gram_band.1 = (bf16[256,1152]{1,0:T(8,128)(2,1)S(1)}, bf16[256,1152]{1,0:T(8,128)(2,1)S(1)}, bf16[256,1152]{1,0:T(8,128)(2,1)S(1)}, bf16[256,1152]{1,0:T(8,128)(2,1)S(1)}, bf16[256,2048]{1,0:T(8,128)(2,1)S(1)}) custom-call(s32[3]{0:T(128)S(1)} %pad_add_fusion.place_ref, bf16[8,16,3584]{2,1,0:T(8,128)(2,1)S(1)} %all-to-all-done.mine_ref, ...), custom_call_target="tpu_custom_call" | custom-call | tf_op jit(solution)/shard_map/gram_band/pallas_call | solution.py:154
  43.8 1.6 %collective-permute-start.8 = (bf16[256,1152]{1,0:T(8,128)(2,1)S(1)}, bf16[256,1152]{1,0:T(8,128)(2,1)S(1)}, u32[]{:S(2)}, u32[]{:S(2)}) collective-permute-start(bf16[256,1152]{1,0:T(8,128)(2,1)S(1)} %get-tuple-element.48), channel_id=1, source_target_pairs={{0,64},{8,24},{16,80},{24,40},{32,96},{40,56},{48,112},{56,8},{64,... | collective-permute-start | bytes 1769480 | tf_op jit(solution)/shard_map/ppermute | solution.py:289
  46.5 2.2 %collective-permute-start.10 = (bf16[256,1152]{1,0:T(8,128)(2,1)S(1)}, bf16[256,1152]{1,0:T(8,128)(2,1)S(1)}, u32[]{:S(2)}, u32[]{:S(2)}) collective-permute-start(bf16[256,1152]{1,0:T(8,128)(2,1)S(1)} %get-tuple-element.50), channel_id=1, source_target_pairs={{0,192},{8,56},{16,208},{24,8},{32,224},{40,24},{48,240},{56,40},{... | collective-permute-start | bytes 1769480 | tf_op jit(solution)/shard_map/ppermute | solution.py:289
  49.2 4.2 %collective-permute-done.6 = f32[1,64]{1,0:T(1,128)S(1)} collective-permute-done((f32[1,64]{1,0:T(1,128)S(1)}, f32[1,64]{1,0:T(1,128)S(1)}, u32[]{:S(2)}, u32[]{:S(2)}) %collective-permute-start.6) | collective-permute-done | bytes 288 | tf_op jit(solution)/shard_map/ppermute | solution.py:313
  53.4 5.6 %collective-permute-done.7 = f32[1,64]{1,0:T(1,128)S(1)} collective-permute-done((f32[1,64]{1,0:T(1,128)S(1)}, f32[1,64]{1,0:T(1,128)S(1)}, u32[]{:S(2)}, u32[]{:S(2)}) %collective-permute-start.7) | collective-permute-done | bytes 288 | tf_op jit(solution)/shard_map/ppermute | solution.py:313
  59.1 3.6 %collective-permute-done.10.refs_3_ = bf16[256,1152]{1,0:T(8,128)(2,1)S(1)} collective-permute-done((bf16[256,1152]{1,0:T(8,128)(2,1)S(1)}, bf16[256,1152]{1,0:T(8,128)(2,1)S(1)}, u32[]{:S(2)}, u32[]{:S(2)}) %collective-permute-start.10) | collective-permute-done | bytes 589856 | tf_op jit(solution)/shard_map/ppermute | solution.py:289
  63.0 1.7 %collective-permute-start.11 = (bf16[128,1152]{1,0:T(8,128)(2,1)S(1)}, bf16[128,1152]{1,0:T(8,128)(2,1)S(1)}, u32[]{:S(2)}, u32[]{:S(2)}) collective-permute-start(bf16[128,1152]{1,0:T(8,128)(2,1)S(1)} %get-tuple-element.51.refs_0_), channel_id=1, source_target_pairs={{0,16},{8,72},{16,0},{24,88},{32,48},{40,104},{48,32},{56,120},{64... | collective-permute-start | bytes 884744 | tf_op jit(solution)/shard_map/ppermute | solution.py:298
  64.6 2.2 %collective-permute-start.12 = (bf16[128,1152]{1,0:T(8,128)(2,1)S(1)}, bf16[128,1152]{1,0:T(8,128)(2,1)S(1)}, u32[]{:S(2)}, u32[]{:S(2)}) collective-permute-start(bf16[128,1152]{1,0:T(8,128)(2,1)S(1)} %get-tuple-element.52.refs_1_), channel_id=1, source_target_pairs={{0,48},{8,200},{16,32},{24,216},{32,16},{40,232},{48,0},{56,248},{... | collective-permute-start | bytes 884744 | tf_op jit(solution)/shard_map/ppermute | solution.py:298
  66.8 3.0 %collective-permute-done.11.refs_2_ = bf16[128,1152]{1,0:T(8,128)(2,1)S(1)} collective-permute-done((bf16[128,1152]{1,0:T(8,128)(2,1)S(1)}, bf16[128,1152]{1,0:T(8,128)(2,1)S(1)}, u32[]{:S(2)}, u32[]{:S(2)}) %collective-permute-start.11) | collective-permute-done | bytes 294944 | tf_op jit(solution)/shard_map/ppermute | solution.py:298
  69.8 2.8 %collective-permute-done.12.refs_3_ = bf16[128,1152]{1,0:T(8,128)(2,1)S(1)} collective-permute-done((bf16[128,1152]{1,0:T(8,128)(2,1)S(1)}, bf16[128,1152]{1,0:T(8,128)(2,1)S(1)}, u32[]{:S(2)}, u32[]{:S(2)}) %collective-permute-start.12) | collective-permute-done | bytes 294944 | tf_op jit(solution)/shard_map/ppermute | solution.py:298
  72.7 2.3 %collective-permute-start.13 = (bf16[128,1152]{1,0:T(8,128)(2,1)S(1)}, bf16[128,1152]{1,0:T(8,128)(2,1)S(1)}, u32[]{:S(2)}, u32[]{:S(2)}) collective-permute-start(bf16[128,1152]{1,0:T(8,128)(2,1)S(1)} %get-tuple-element.53.refs_0_), channel_id=1, source_target_pairs={{0,48},{8,200},{16,32},{24,216},{32,16},{40,232},{48,0},{56,248},{... | collective-permute-start | bytes 884744 | tf_op jit(solution)/shard_map/ppermute | solution.py:298
  75.0 5.7 %collective-permute-done.13.refs_2_ = bf16[128,1152]{1,0:T(8,128)(2,1)S(1)} collective-permute-done((bf16[128,1152]{1,0:T(8,128)(2,1)S(1)}, bf16[128,1152]{1,0:T(8,128)(2,1)S(1)}, u32[]{:S(2)}, u32[]{:S(2)}) %collective-permute-start.13) | collective-permute-done | bytes 294944 | tf_op jit(solution)/shard_map/ppermute | solution.py:298
  80.7 2.2 %collective-permute-done.14.refs_3_ = bf16[128,1152]{1,0:T(8,128)(2,1)S(1)} collective-permute-done((bf16[128,1152]{1,0:T(8,128)(2,1)S(1)}, bf16[128,1152]{1,0:T(8,128)(2,1)S(1)}, u32[]{:S(2)}, u32[]{:S(2)}) %collective-permute-start.14) | collective-permute-done | bytes 294944 | tf_op jit(solution)/shard_map/ppermute | solution.py:298
  84.1 2.6 %collective-permute-start.18 = (bf16[256,1152]{1,0:T(8,128)(2,1)S(1)}, bf16[256,1152]{1,0:T(8,128)(2,1)S(1)}, u32[]{:S(2)}, u32[]{:S(2)}) collective-permute-start(bf16[256,1152]{1,0:T(8,128)(2,1)S(1)} %add_pairs.3.refs_0_), channel_id=1, source_target_pairs={{0,192},{8,56},{16,208},{24,8},{32,224},{40,24},{48,240},{56,40},{... | collective-permute-start | bytes 1769480 | tf_op jit(solution)/shard_map/ppermute | solution.py:289
  87.3 6.9 %collective-permute-done.16 = f32[1,64]{1,0:T(1,128)S(1)} collective-permute-done((f32[1,64]{1,0:T(1,128)S(1)}, f32[1,64]{1,0:T(1,128)S(1)}, u32[]{:S(2)}, u32[]{:S(2)}) %collective-permute-start.16) | collective-permute-done | bytes 288 | tf_op jit(solution)/shard_map/ppermute | solution.py:313
  94.6 5.6 %collective-permute-done.18.refs_3_ = bf16[256,1152]{1,0:T(8,128)(2,1)S(1)} collective-permute-done((bf16[256,1152]{1,0:T(8,128)(2,1)S(1)}, bf16[256,1152]{1,0:T(8,128)(2,1)S(1)}, u32[]{:S(2)}, u32[]{:S(2)}) %collective-permute-start.18) | collective-permute-done | bytes 589856 | tf_op jit(solution)/shard_map/ppermute | solution.py:289
  104.0 10.3 %finish.1 = bf16[8,16,3584]{2,1,0:T(8,128)(2,1)} custom-call(s32[3]{0:T(128)S(1)} %pad_add_fusion.place_ref, bf16[256,2048]{1,0:T(8,128)(2,1)S(1)} %get-tuple-element.42.x_ref, bf16[256,1152]{1,0:T(8,128)(2,1)S(1)} %add_pairs.3.refs_0_, bf16[256,1152]{1,0:T(8,128)(2,1)S(1)} %collective-permute-done.17.refs_1_, ...), custom_call_target="tpu_custom_call" | custom-call | tf_op jit(solution)/shard_map/finish/pallas_call | solution.py:256
  114.3 3.7 %all-to-all-start.1 = ((bf16[8,16,3584]{2,1,0:T(8,128)(2,1)}), bf16[8,16,3584]{2,1,0:T(8,128)(2,1)S(1)}, u32[]{:S(2)}, u32[]{:S(2)}) async-start(bf16[8,16,3584]{2,1,0:T(8,128)(2,1)} %finish.1), calls=%async_computation.1 | async-start | bytes 1835008 | tf_op jit(solution)/shard_map/all_to_all | solution.py:343
  119.7 24.7 %all-to-all-done.1.packed_ref = bf16[8,16,3584]{2,1,0:T(8,128)(2,1)S(1)} async-done(((bf16[8,16,3584]{2,1,0:T(8,128)(2,1)}), bf16[8,16,3584]{2,1,0:T(8,128)(2,1)S(1)}, u32[]{:S(2)}, u32[]{:S(2)}) %all-to-all-start.1) | async-done | bytes 917536 | tf_op jit(solution)/shard_map/all_to_all | solution.py:343
  144.4 1.7 %spread_step.1 = bf16[28,8,2048]{2,1,0:T(8,128)(2,1)} custom-call(bf16[8,16,3584]{2,1,0:T(8,128)(2,1)S(1)} %all-to-all-done.1.packed_ref), custom_call_target="tpu_custom_call" | custom-call | tf_op jit(solution)/shard_map/spread_step/pallas_call | solution.py:112
  (52 shorter events, 11.5 us)
Async XLA Ops:
  0.6 12.4 %copy-start.3 = (f32[1,64]{1,0:T(1,128)S(1)}, f32[1,64]{1,0:T(1,128)}, u32[]{:S(2)}) copy-start(f32[1,64]{1,0:T(1,128)} %param.7) | copy-start | bytes 772
  4.5 25.2 %copy-start = (f32[8,28,2048]{2,0,1:T(8,128)S(1)}, f32[8,28,2048]{2,0,1:T(8,128)}, u32[]{:S(2)}) copy-start(f32[8,28,2048]{2,0,1:T(8,128)} %param.6) | copy-start | bytes 5505028
  4.5 34.5 %all-to-all-start = ((bf16[8,16,3584]{2,1,0:T(8,128)(2,1)}), bf16[8,16,3584]{2,1,0:T(8,128)(2,1)S(1)}, u32[]{:S(2)}, u32[]{:S(2)}) async-start(bf16[8,16,3584]{2,1,0:T(8,128)(2,1)} %find_direction.1), calls=%async_computation | async-start | bytes 1835008 | tf_op jit(solution)/shard_map/all_to_all | solution.py:322
  13.1 1.2 collective-permute-start
  14.3 3.5 %collective-permute-start.1 = (f32[1,64]{1,0:T(1,128)S(1)}, f32[1,64]{1,0:T(1,128)S(1)}, u32[]{:S(2)}, u32[]{:S(2)}) collective-permute-start(f32[1,64]{1,0:T(1,128)S(1)} %max.24), channel_id=1, source_target_pairs={{0,64},{64,128},{128,192},{192,0},{1,65},{65,129},{129,193},{193,1... | collective-permute-start | bytes 776 | tf_op jit(solution)/shard_map/ppermute | solution.py:313
  17.8 5.0 %collective-permute-start.2 = (f32[1,64]{1,0:T(1,128)S(1)}, f32[1,64]{1,0:T(1,128)S(1)}, u32[]{:S(2)}, u32[]{:S(2)}) collective-permute-start(f32[1,64]{1,0:T(1,128)S(1)} %max.25), channel_id=1, source_target_pairs={{0,128},{64,192},{128,0},{192,64},{1,129},{65,193},{129,1},{193,65... | collective-permute-start | bytes 776 | tf_op jit(solution)/shard_map/ppermute | solution.py:313
  22.9 4.8 %collective-permute-start.3 = (f32[1,64]{1,0:T(1,128)S(1)}, f32[1,64]{1,0:T(1,128)S(1)}, u32[]{:S(2)}, u32[]{:S(2)}) collective-permute-start(f32[1,64]{1,0:T(1,128)S(1)} %max.26), channel_id=1, source_target_pairs={{0,16},{16,32},{32,48},{48,0},{1,17},{17,33},{33,49},{49,1},{2,18}... | collective-permute-start | bytes 776 | tf_op jit(solution)/shard_map/ppermute | solution.py:313
  27.6 5.0 %collective-permute-start.4 = (f32[1,64]{1,0:T(1,128)S(1)}, f32[1,64]{1,0:T(1,128)S(1)}, u32[]{:S(2)}, u32[]{:S(2)}) collective-permute-start(f32[1,64]{1,0:T(1,128)S(1)} %max.27), channel_id=1, source_target_pairs={{0,32},{16,48},{32,0},{48,16},{1,33},{17,49},{33,1},{49,17},{2,34}... | collective-permute-start | bytes 776 | tf_op jit(solution)/shard_map/ppermute | solution.py:313
  39.0 2.5 %collective-permute-start.5 = (bf16[8,16,3584]{2,1,0:T(8,128)(2,1)S(1)}, bf16[8,16,3584]{2,1,0:T(8,128)(2,1)S(1)}, u32[]{:S(2)}, u32[]{:S(2)}) collective-permute-start(bf16[8,16,3584]{2,1,0:T(8,128)(2,1)S(1)} %all-to-all-done.mine_ref), channel_id=1, source_target_pairs={{0,8},{8,0},{1,9},{9,1},{2,10},{10,2},{3,11},{11,3},{4,12},{12,4},... | collective-permute-start | bytes 2752520 | tf_op jit(solution)/shard_map/ppermute | solution.py:309
  43.8 15.3 %collective-permute-start.8 = (bf16[256,1152]{1,0:T(8,128)(2,1)S(1)}, bf16[256,1152]{1,0:T(8,128)(2,1)S(1)}, u32[]{:S(2)}, u32[]{:S(2)}) collective-permute-start(bf16[256,1152]{1,0:T(8,128)(2,1)S(1)} %get-tuple-element.48), channel_id=1, source_target_pairs={{0,64},{8,24},{16,80},{24,40},{32,96},{40,56},{48,112},{56,8},{64,... | collective-permute-start | bytes 1769480 | tf_op jit(solution)/shard_map/ppermute | solution.py:289
  45.4 13.7 %collective-permute-start.9 = (bf16[256,1152]{1,0:T(8,128)(2,1)S(1)}, bf16[256,1152]{1,0:T(8,128)(2,1)S(1)}, u32[]{:S(2)}, u32[]{:S(2)}) collective-permute-start(bf16[256,1152]{1,0:T(8,128)(2,1)S(1)} %get-tuple-element.49), channel_id=1, source_target_pairs={{0,128},{8,40},{16,144},{24,56},{32,160},{40,8},{48,176},{56,24},{... | collective-permute-start | bytes 1769480 | tf_op jit(solution)/shard_map/ppermute | solution.py:289
  46.5 16.2 %collective-permute-start.10 = (bf16[256,1152]{1,0:T(8,128)(2,1)S(1)}, bf16[256,1152]{1,0:T(8,128)(2,1)S(1)}, u32[]{:S(2)}, u32[]{:S(2)}) collective-permute-start(bf16[256,1152]{1,0:T(8,128)(2,1)S(1)} %get-tuple-element.50), channel_id=1, source_target_pairs={{0,192},{8,56},{16,208},{24,8},{32,224},{40,24},{48,240},{56,40},{... | collective-permute-start | bytes 1769480 | tf_op jit(solution)/shard_map/ppermute | solution.py:289
  48.6 4.8 %collective-permute-start.6 = (f32[1,64]{1,0:T(1,128)S(1)}, f32[1,64]{1,0:T(1,128)S(1)}, u32[]{:S(2)}, u32[]{:S(2)}) collective-permute-start(f32[1,64]{1,0:T(1,128)S(1)} %max.28), channel_id=1, source_target_pairs={{0,1},{1,2},{2,3},{3,4},{4,5},{5,6},{6,7},{7,0},{8,9},{9,10},{10,1... | collective-permute-start | bytes 776 | tf_op jit(solution)/shard_map/ppermute | solution.py:313
  53.4 5.7 %collective-permute-start.7 = (f32[1,64]{1,0:T(1,128)S(1)}, f32[1,64]{1,0:T(1,128)S(1)}, u32[]{:S(2)}, u32[]{:S(2)}) collective-permute-start(f32[1,64]{1,0:T(1,128)S(1)} %max.29), channel_id=1, source_target_pairs={{0,2},{1,3},{2,4},{3,5},{4,6},{5,7},{6,0},{7,1},{8,10},{9,11},{10,... | collective-permute-start | bytes 776 | tf_op jit(solution)/shard_map/ppermute | solution.py:313
  63.0 6.8 %collective-permute-start.11 = (bf16[128,1152]{1,0:T(8,128)(2,1)S(1)}, bf16[128,1152]{1,0:T(8,128)(2,1)S(1)}, u32[]{:S(2)}, u32[]{:S(2)}) collective-permute-start(bf16[128,1152]{1,0:T(8,128)(2,1)S(1)} %get-tuple-element.51.refs_0_), channel_id=1, source_target_pairs={{0,16},{8,72},{16,0},{24,88},{32,48},{40,104},{48,32},{56,120},{64... | collective-permute-start | bytes 884744 | tf_op jit(solution)/shard_map/ppermute | solution.py:298
  64.6 7.9 %collective-permute-start.12 = (bf16[128,1152]{1,0:T(8,128)(2,1)S(1)}, bf16[128,1152]{1,0:T(8,128)(2,1)S(1)}, u32[]{:S(2)}, u32[]{:S(2)}) collective-permute-start(bf16[128,1152]{1,0:T(8,128)(2,1)S(1)} %get-tuple-element.52.refs_1_), channel_id=1, source_target_pairs={{0,48},{8,200},{16,32},{24,216},{32,16},{40,232},{48,0},{56,248},{... | collective-permute-start | bytes 884744 | tf_op jit(solution)/shard_map/ppermute | solution.py:298
  72.7 8.0 %collective-permute-start.13 = (bf16[128,1152]{1,0:T(8,128)(2,1)S(1)}, bf16[128,1152]{1,0:T(8,128)(2,1)S(1)}, u32[]{:S(2)}, u32[]{:S(2)}) collective-permute-start(bf16[128,1152]{1,0:T(8,128)(2,1)S(1)} %get-tuple-element.53.refs_0_), channel_id=1, source_target_pairs={{0,48},{8,200},{16,32},{24,216},{32,16},{40,232},{48,0},{56,248},{... | collective-permute-start | bytes 884744 | tf_op jit(solution)/shard_map/ppermute | solution.py:298
  75.0 7.9 %collective-permute-start.14 = (bf16[128,1152]{1,0:T(8,128)(2,1)S(1)}, bf16[128,1152]{1,0:T(8,128)(2,1)S(1)}, u32[]{:S(2)}, u32[]{:S(2)}) collective-permute-start(bf16[128,1152]{1,0:T(8,128)(2,1)S(1)} %get-tuple-element.54.refs_1_), channel_id=1, source_target_pairs={{0,16},{8,72},{16,0},{24,88},{32,48},{40,104},{48,32},{56,120},{64... | collective-permute-start | bytes 884744 | tf_op jit(solution)/shard_map/ppermute | solution.py:298
  83.1 11.6 %collective-permute-start.15 = (bf16[256,1152]{1,0:T(8,128)(2,1)S(1)}, bf16[256,1152]{1,0:T(8,128)(2,1)S(1)}, u32[]{:S(2)}, u32[]{:S(2)}) collective-permute-start(bf16[256,1152]{1,0:T(8,128)(2,1)S(1)} %add_pairs.3.refs_0_), channel_id=1, source_target_pairs={{0,128},{8,40},{16,144},{24,56},{32,160},{40,8},{48,176},{56,24},{... | collective-permute-start | bytes 1769480 | tf_op jit(solution)/shard_map/ppermute | solution.py:289
  84.1 16.2 %collective-permute-start.18 = (bf16[256,1152]{1,0:T(8,128)(2,1)S(1)}, bf16[256,1152]{1,0:T(8,128)(2,1)S(1)}, u32[]{:S(2)}, u32[]{:S(2)}) collective-permute-start(bf16[256,1152]{1,0:T(8,128)(2,1)S(1)} %add_pairs.3.refs_0_), channel_id=1, source_target_pairs={{0,192},{8,56},{16,208},{24,8},{32,224},{40,24},{48,240},{56,40},{... | collective-permute-start | bytes 1769480 | tf_op jit(solution)/shard_map/ppermute | solution.py:289
  86.7 14.2 %collective-permute-start.17 = (bf16[256,1152]{1,0:T(8,128)(2,1)S(1)}, bf16[256,1152]{1,0:T(8,128)(2,1)S(1)}, u32[]{:S(2)}, u32[]{:S(2)}) collective-permute-start(bf16[256,1152]{1,0:T(8,128)(2,1)S(1)} %add_pairs.3.refs_0_), channel_id=1, source_target_pairs={{0,64},{8,24},{16,80},{24,40},{32,96},{40,56},{48,112},{56,8},{64,... | collective-permute-start | bytes 1769480 | tf_op jit(solution)/shard_map/ppermute | solution.py:289
  86.7 7.4 %collective-permute-start.16 = (f32[1,64]{1,0:T(1,128)S(1)}, f32[1,64]{1,0:T(1,128)S(1)}, u32[]{:S(2)}, u32[]{:S(2)}) collective-permute-start(f32[1,64]{1,0:T(1,128)S(1)} %max.30), channel_id=1, source_target_pairs={{0,4},{1,5},{2,6},{3,7},{4,0},{5,1},{6,2},{7,3},{8,12},{9,13},{10,... | collective-permute-start | bytes 776 | tf_op jit(solution)/shard_map/ppermute | solution.py:313
  94.6 8.5 %collective-permute-start.19 = (bf16[256,1152]{1,0:T(8,128)(2,1)S(1)}, bf16[256,1152]{1,0:T(8,128)(2,1)S(1)}, u32[]{:S(2)}, u32[]{:S(2)}) collective-permute-start(bf16[256,1152]{1,0:T(8,128)(2,1)S(1)} %add_pairs.3.refs_0_), channel_id=1, source_target_pairs={{0,8},{8,0},{1,9},{9,1},{2,10},{10,2},{3,11},{11,3},{4,12},{12,4},... | collective-permute-start | bytes 1769480 | tf_op jit(solution)/shard_map/ppermute | solution.py:309
  100.3 2.0 %collective-permute-start.22 = (bf16[256,1152]{1,0:T(8,128)(2,1)S(1)}, bf16[256,1152]{1,0:T(8,128)(2,1)S(1)}, u32[]{:S(2)}, u32[]{:S(2)}) collective-permute-start(bf16[256,1152]{1,0:T(8,128)(2,1)S(1)} %collective-permute-done.18.refs_3_), channel_id=1, source_target_pairs={{0,8},{8,0},{1,9},{9,1},{2,10},{10,2},{3,11},{11,3},{4,12},{12,4},... | collective-permute-start | bytes 1769480 | tf_op jit(solution)/shard_map/ppermute | solution.py:309
  100.9 2.2 %collective-permute-start.20 = (bf16[256,1152]{1,0:T(8,128)(2,1)S(1)}, bf16[256,1152]{1,0:T(8,128)(2,1)S(1)}, u32[]{:S(2)}, u32[]{:S(2)}) collective-permute-start(bf16[256,1152]{1,0:T(8,128)(2,1)S(1)} %collective-permute-done.17.refs_1_), channel_id=1, source_target_pairs={{0,8},{8,0},{1,9},{9,1},{2,10},{10,2},{3,11},{11,3},{4,12},{12,4},... | collective-permute-start | bytes 1769480 | tf_op jit(solution)/shard_map/ppermute | solution.py:309
  100.9 3.1 %collective-permute-start.21 = (bf16[256,1152]{1,0:T(8,128)(2,1)S(1)}, bf16[256,1152]{1,0:T(8,128)(2,1)S(1)}, u32[]{:S(2)}, u32[]{:S(2)}) collective-permute-start(bf16[256,1152]{1,0:T(8,128)(2,1)S(1)} %collective-permute-done.15.refs_2_), channel_id=1, source_target_pairs={{0,8},{8,0},{1,9},{9,1},{2,10},{10,2},{3,11},{11,3},{4,12},{12,4},... | collective-permute-start | bytes 1769480 | tf_op jit(solution)/shard_map/ppermute | solution.py:309
  114.3 4.1 %copy-start.2 = (bf16[16,1024]{1,0:T(8,128)(2,1)S(1)}, bf16[16,1024]{1,0:T(8,128)(2,1)}, u32[]{:S(2)}) copy-start(bf16[16,1024]{1,0:T(8,128)(2,1)} %param.9) | copy-start | bytes 98308
  114.3 4.7 %copy-start.1 = (bf16[48,1536]{1,0:T(8,128)(2,1)S(1)}, bf16[48,1536]{1,0:T(8,128)(2,1)}, u32[]{:S(2)}) copy-start(bf16[48,1536]{1,0:T(8,128)(2,1)} %param.8) | copy-start | bytes 442372
  114.3 30.1 %all-to-all-start.1 = ((bf16[8,16,3584]{2,1,0:T(8,128)(2,1)}), bf16[8,16,3584]{2,1,0:T(8,128)(2,1)S(1)}, u32[]{:S(2)}, u32[]{:S(2)}) async-start(bf16[8,16,3584]{2,1,0:T(8,128)(2,1)} %finish.1), calls=%async_computation.1 | async-start | bytes 1835008 | tf_op jit(solution)/shard_map/all_to_all | solution.py:343
